TPU v7x, 32 devices: a whole 2x2x4 slice. The times are simulated.
32 devices in a mesh: groups: 2 (over y), ctx: 4 (over z), dp: 2 (over x), head: 2 (over core).
Axes of the slice: x: 2, y: 2, z: 4, core: 2. Of those that a mesh axis runs over, the one named last changes fastest.
Arguments:
- queries: bfloat16 [4, 2048, 32, 128], P(('groups', 'dp'), 'ctx', 'head'), parts along dimension 0, may hold values from -128 to 128
- key_states: bfloat16 [4, 2048, 4, 128], P(('groups', 'dp'), 'ctx', 'head'), parts along dimension 0, may hold values from -7 to 7
- value_states: bfloat16 [4, 2048, 4, 128], P(('groups', 'dp'), 'ctx', 'head'), parts along dimension 0, may hold values from -6 to 6
- teacher_out: bfloat16 [4, 2048, 32, 128], P(('groups', 'dp'), 'ctx', 'head'), parts along dimension 0, may hold values from -6 to 6
- selection: int32 [4, 32, 4, 16], P(('groups', 'dp'), 'ctx', 'head'), parts along dimension 0, may hold values from -1 to 31, as said below
- compress_keys: float32 [4, 64, 128], P('head'), may hold values from -0.75 to 0.75
- compress_values: float32 [4, 64, 128], P('head'), may hold values from -0.75 to 0.75
- gate_weights: float32 [32, 2, 128], P('head'), may hold values from -0.5 to 0.5
Outputs:
- key_grad: bfloat16 [4, 2048, 4, 128], P(('groups', 'dp'), 'ctx', 'head'), parts along dimension 0
- value_grad: bfloat16 [4, 2048, 4, 128], P(('groups', 'dp'), 'ctx', 'head'), parts along dimension 0
- compress_key_grad: float32 [8, 64, 128], P(('groups', 'head')), parts along dimension 0
- compress_value_grad: float32 [8, 64, 128], P(('groups', 'head')), parts along dimension 0
- gate_grad: float32 [64, 2, 128], P(('groups', 'head')), parts along dimension 0
There are 2 independent parts, one for each index of `groups`. A program takes and returns all parts, laid end to end along the dimension named above; an argument that names none is the same for every part. Nothing has to cross between parts.
Inputs may be any that keep to these rules, and one draw needn't show every extreme that they name: `selection`: each list of query block j and key-value head names distinct blocks up to j, always j and 0; unused slots hold -1 and come last. Of the blocks named by the query blocks of one index of ctx, for one context and key-value head, those held by another index number at most 4 for each other index; on the last index of ctx exactly 4 for every other index.
All inputs are finite; a program needn't handle non-finite values.
Results may differ from a plain program's by a relative error of at most 0.003.
The roundings to bfloat16 on the way count: a program that leaves them out, or rounds other values in their place, can miss the bound.
Values may be sent and summed in bfloat16 or wider, within the bound.
A program may use at most 128 MiB of HBM per device.

v0:
```python
import math

import jax
import jax.numpy as jnp
from jax import lax
from jax.sharding import PartitionSpec as P

HIGHEST = lax.Precision.HIGHEST
MASKED = -1e30


def masked_softmax(scores, usable):
    peaks = jnp.max(jnp.where(usable, scores, MASKED), axis=-1, keepdims=True)
    raised = jnp.where(usable, jnp.exp(jnp.where(usable, scores, peaks) - peaks), 0.0)
    return raised / jnp.sum(raised, axis=-1, keepdims=True)


def branch_grads(weights, rounded, back_rounded, queried, piece_values, factor):
    weight_grad = jnp.einsum(
        "tgnd,gkd->gtnk", back_rounded, piece_values, preferred_element_type=jnp.float32
    )
    row_total = jnp.sum(weights * weight_grad, axis=-1, keepdims=True)
    score_grad = (factor * weights * (weight_grad - row_total)).astype(jnp.bfloat16)
    value_part = jnp.einsum(
        "gtnk,tgnd->gkd", rounded, back_rounded, preferred_element_type=jnp.float32
    )
    key_part = jnp.einsum("gtnk,tgnd->gkd", score_grad, queried, preferred_element_type=jnp.float32)
    return (key_part, value_part)


def attend_block(
    queried,
    teacher_rows,
    piece_keys,
    piece_values,
    key_usable,
    comp_keys,
    comp_values,
    comp_usable,
    gate_grouped,
):
    factor = queried.shape[-1] ** (-0.5)
    sel_scores = (
        jnp.einsum("tgnd,gkd->gtnk", queried, piece_keys, preferred_element_type=jnp.float32)
        * factor
    )
    sel_weights = masked_softmax(sel_scores, key_usable[:, :, None, :])
    sel_rounded = sel_weights.astype(jnp.bfloat16)
    sel_out = jnp.einsum(
        "gtnk,gkd->tgnd", sel_rounded, piece_values, preferred_element_type=jnp.float32
    )
    comp_scores = (
        jnp.einsum("tgnd,gkd->gtnk", queried, comp_keys, preferred_element_type=jnp.float32)
        * factor
    )
    comp_weights = masked_softmax(comp_scores, comp_usable[None, None, None, :])
    comp_rounded = comp_weights.astype(jnp.bfloat16)
    comp_out = jnp.einsum(
        "gtnk,gkd->tgnd", comp_rounded, comp_values, preferred_element_type=jnp.float32
    )
    query_wide = queried.astype(jnp.float32)
    gate_logits = jnp.einsum("tgnd,gnrd->tgnr", query_wide, gate_grouped, precision=HIGHEST)
    gates = jax.nn.sigmoid(gate_logits)
    mixed = gates[..., 0:1] * comp_out + gates[..., 1:2] * sel_out
    error = mixed - teacher_rows.astype(jnp.float32)
    gate_terms = jnp.stack(
        [jnp.sum(error * comp_out, axis=-1), jnp.sum(error * sel_out, axis=-1)], axis=-1
    ) * (gates * (1.0 - gates))
    gate_part = jnp.einsum("tgnr,tgnd->gnrd", gate_terms, query_wide, precision=HIGHEST)
    sel_back = (gates[..., 1:2] * error).astype(jnp.bfloat16)
    comp_back = (gates[..., 0:1] * error).astype(jnp.bfloat16)
    sel_key, sel_value = branch_grads(
        sel_weights, sel_rounded, sel_back, queried, piece_values, factor
    )
    comp_key, comp_value = branch_grads(
        comp_weights, comp_rounded, comp_back, queried, comp_values, factor
    )
    return (sel_key, sel_value, comp_key, comp_value, gate_part)


def on_device(
    queries,
    key_states,
    value_states,
    teacher_out,
    selection,
    compress_keys,
    compress_values,
    gate_weights,
):
    ctx_count = lax.axis_size("ctx")
    my_index = lax.axis_index("ctx")
    tokens_dev = key_states.shape[1]
    kv_heads = key_states.shape[2]
    head_dim = key_states.shape[3]
    span = compress_keys.shape[1]
    own_blocks = tokens_dev // span
    all_blocks = own_blocks * ctx_count
    group = queries.shape[2] // kv_heads
    picks = selection.shape[3]
    key_blocks = key_states[0].reshape(own_blocks, span, kv_heads, head_dim)
    value_blocks = value_states[0].reshape(own_blocks, span, kv_heads, head_dim)
    comp_key_local = jnp.einsum(
        "bugd,gud->bgd", key_blocks.astype(jnp.float32), compress_keys, precision=HIGHEST
    ).astype(jnp.bfloat16)
    comp_value_local = jnp.einsum(
        "bugd,gud->bgd", value_blocks.astype(jnp.float32), compress_values, precision=HIGHEST
    ).astype(jnp.bfloat16)
    comp_keys, comp_values = (
        lax.all_gather(comp_key_local, "ctx", axis=0, tiled=True),
        lax.all_gather(comp_value_local, "ctx", axis=0, tiled=True),
    )
    comp_keys = comp_keys.transpose(1, 0, 2)
    comp_values = comp_values.transpose(1, 0, 2)
    chosen_all = selection[0]
    usable_all = chosen_all >= 0
    key_pieces_local = key_blocks.transpose(2, 0, 1, 3)
    value_pieces_local = value_blocks.transpose(2, 0, 1, 3)
    capacity = own_blocks // 2
    holder = jnp.where(usable_all, chosen_all // own_blocks, my_index)
    within = jnp.where(usable_all, chosen_all % own_blocks, 0)
    remote = usable_all & (holder != my_index)
    match_table = (chosen_all[..., None] == jnp.arange(all_blocks)) & remote[..., None]
    present = (
        jnp.any(match_table, axis=(0, 2)).astype(jnp.int32).reshape(kv_heads, ctx_count, own_blocks)
    )
    slot_rank = jnp.cumsum(present, axis=-1) - present
    slot_hit = (present[..., None] == 1) & (slot_rank[..., None] == jnp.arange(capacity))
    request = jnp.sum(slot_hit.astype(jnp.int32) * jnp.arange(own_blocks)[:, None], axis=2)
    asked = lax.all_to_all(
        request.transpose(1, 0, 2), "ctx", split_axis=0, concat_axis=0, tiled=True
    )
    head_pick = jnp.arange(kv_heads)[None, :, None]
    send_keys = key_pieces_local[head_pick, asked]
    send_values = value_pieces_local[head_pick, asked]
    got_keys, got_values = (
        lax.all_to_all(send_keys, "ctx", split_axis=0, concat_axis=0, tiled=True),
        lax.all_to_all(send_values, "ctx", split_axis=0, concat_axis=0, tiled=True),
    )
    remote_slots = ctx_count * capacity
    key_lookup = jnp.concatenate(
        [
            got_keys.transpose(1, 0, 2, 3, 4).reshape(kv_heads, remote_slots, span, head_dim),
            key_pieces_local,
        ],
        axis=1,
    )
    value_lookup = jnp.concatenate(
        [
            got_values.transpose(1, 0, 2, 3, 4).reshape(kv_heads, remote_slots, span, head_dim),
            value_pieces_local,
        ],
        axis=1,
    )
    rank_flat = slot_rank.reshape(kv_heads, all_blocks)
    remote_slot = holder * capacity + jnp.sum(
        match_table.astype(jnp.int32) * rank_flat[None, :, None, :], axis=-1
    )
    lookup_all = jnp.where(remote, remote_slot, remote_slots + within)
    slots = key_lookup.shape[1]
    query_blocks = queries[0].reshape(own_blocks, span, kv_heads, group, head_dim)
    teacher_blocks = teacher_out[0].reshape(own_blocks, span, kv_heads, group, head_dim)
    current_blocks = my_index * own_blocks + jnp.arange(own_blocks)
    head_range = jnp.arange(kv_heads)[:, None]
    offsets = jnp.arange(span)
    causal = offsets[None, :] <= offsets[:, None]
    gate_grouped = gate_weights.reshape(kv_heads, group, 2, head_dim)
    block_range = jnp.arange(all_blocks)

    def advance(carry, items):
        key_acc, value_acc, comp_key_acc, comp_value_acc, gate_acc = carry
        queried, teacher_rows, chosen, lookup, current = items
        usable = chosen >= 0
        piece_keys = key_lookup[head_range, lookup].reshape(kv_heads, picks * span, head_dim)
        piece_values = value_lookup[head_range, lookup].reshape(kv_heads, picks * span, head_dim)
        own_block = chosen == current
        key_usable = usable[:, None, :, None] & (
            jnp.logical_not(own_block)[:, None, :, None] | causal[None, :, None, :]
        )
        key_usable = key_usable.reshape(kv_heads, span, picks * span)
        comp_usable = block_range <= current
        sel_key, sel_value, comp_key, comp_value, gate_part = attend_block(
            queried,
            teacher_rows,
            piece_keys,
            piece_values,
            key_usable,
            comp_keys,
            comp_values,
            comp_usable,
            gate_grouped,
        )
        key_acc = key_acc.at[head_range, lookup].add(
            sel_key.reshape(kv_heads, picks, span, head_dim)
        )
        value_acc = value_acc.at[head_range, lookup].add(
            sel_value.reshape(kv_heads, picks, span, head_dim)
        )
        return (
            (
                key_acc,
                value_acc,
                comp_key_acc + comp_key,
                comp_value_acc + comp_value,
                gate_acc + gate_part,
            ),
            None,
        )

    start = (
        jnp.zeros((kv_heads, slots, span, head_dim), jnp.float32),
        jnp.zeros((kv_heads, slots, span, head_dim), jnp.float32),
        jnp.zeros((kv_heads, all_blocks, head_dim), jnp.float32),
        jnp.zeros((kv_heads, all_blocks, head_dim), jnp.float32),
        jnp.zeros((kv_heads, group, 2, head_dim), jnp.float32),
    )
    finish, unused = lax.scan(
        advance, start, (query_blocks, teacher_blocks, chosen_all, lookup_all, current_blocks)
    )
    key_acc, value_acc, comp_key_acc, comp_value_acc, gate_acc = finish
    back_keys = (
        key_acc[:, :remote_slots]
        .reshape(kv_heads, ctx_count, capacity, span, head_dim)
        .transpose(1, 0, 2, 3, 4)
    )
    back_values = (
        value_acc[:, :remote_slots]
        .reshape(kv_heads, ctx_count, capacity, span, head_dim)
        .transpose(1, 0, 2, 3, 4)
    )
    returned_keys, returned_values = (
        lax.all_to_all(
            back_keys.astype(jnp.bfloat16), "ctx", split_axis=0, concat_axis=0, tiled=True
        ).astype(back_keys.dtype),
        lax.all_to_all(
            back_values.astype(jnp.bfloat16), "ctx", split_axis=0, concat_axis=0, tiled=True
        ).astype(back_values.dtype),
    )
    piece_key_grad = key_acc[:, remote_slots:].at[head_pick, asked].add(returned_keys)
    piece_value_grad = value_acc[:, remote_slots:].at[head_pick, asked].add(returned_values)
    comp_key_own, comp_value_own = (
        lax.psum_scatter(comp_key_acc, "ctx", scatter_dimension=1, tiled=True),
        lax.psum_scatter(comp_value_acc, "ctx", scatter_dimension=1, tiled=True),
    )
    key_total = piece_key_grad + compress_keys[:, None, :, :] * comp_key_own[:, :, None, :]
    value_total = piece_value_grad + compress_values[:, None, :, :] * comp_value_own[:, :, None, :]
    key_grad = (
        key_total.transpose(1, 2, 0, 3)
        .reshape(tokens_dev, kv_heads, head_dim)
        .astype(jnp.bfloat16)[None]
    )
    value_grad = (
        value_total.transpose(1, 2, 0, 3)
        .reshape(tokens_dev, kv_heads, head_dim)
        .astype(jnp.bfloat16)[None]
    )
    weight_key = jnp.einsum(
        "gbd,bugd->gud", comp_key_own, key_blocks.astype(jnp.float32), precision=HIGHEST
    )
    weight_value = jnp.einsum(
        "gbd,bugd->gud", comp_value_own, value_blocks.astype(jnp.float32), precision=HIGHEST
    )
    summed = lax.psum(
        (weight_key, weight_value, gate_acc.reshape(kv_heads * group, 2, head_dim)), ("ctx", "dp")
    )
    divisor = math.sqrt(lax.axis_size("dp") * ctx_count * tokens_dev)
    return (key_grad, value_grad, summed[0] / divisor, summed[1] / divisor, summed[2] / divisor)


def solution(mesh):
    placed = (
        P(("groups", "dp"), "ctx", "head", None),
        P(("groups", "dp"), "ctx", "head", None),
        P(("groups", "dp"), "ctx", "head", None),
        P(("groups", "dp"), "ctx", "head", None),
        P(("groups", "dp"), "ctx", "head", None),
        P("head", None, None),
        P("head", None, None),
        P("head", None, None),
    )
    return jax.shard_map(
        on_device,
        mesh=mesh,
        in_specs=placed,
        out_specs=(
            P(("groups", "dp"), "ctx", "head", None),
            P(("groups", "dp"), "ctx", "head", None),
            P(("groups", "head"), None, None),
            P(("groups", "head"), None, None),
            P(("groups", "head"), None, None),
        ),
        check_vma=False,
    )
```

profile of v0, /device:TPU:0, one launch (start us, length us, event | category | flops | bytes accessed | tf_op | source)
XLA Modules:
  0.0 619.9 jit_solution(3375949463575268601)
XLA Ops:
  10.1 6.3 %all-to-all-start = ((s32[4,2,4]{2,1,0:T(2,128)}), s32[4,2,4]{2,1,0:T(2,128)S(1)}, u32[]{:S(2)}, u32[]{:S(2)}) async-start(s32[4,2,4]{2,1,0:T(2,128)} %copy.121), calls=%async_computation | async-start | bytes 8192 | tf_op jit(solution)/shard_map/all_to_all | solution.py:130
  17.4 4.6 all-to-all-done
  23.6 3.5 all-to-all-start.2
  29.1 17.2 %all_gather.6 = bf16[32,2,128]{2,0,1:T(8,128)(2,1)} all-gather(bf16[8,2,128]{2,0,1:T(8,128)(2,1)S(1)} %bitcast.274), channel_id=1, replica_groups=mesh['groups'=2,'ctx'=4,'dp'=2,'head'=2] {'ctx'}, dimensions={0}, use_global_device_ids=true | all-gather | bytes 20480 | tf_op jit(solution)/shard_map/all_gather | solution.py:110
  47.8 3.5 all-to-all-start.1
  51.4 17.6 %all_gather.7 = bf16[32,2,128]{2,0,1:T(8,128)(2,1)} all-gather(bf16[8,2,128]{2,0,1:T(8,128)(2,1)S(1)} %bitcast.275), channel_id=1, replica_groups=mesh['groups'=2,'ctx'=4,'dp'=2,'head'=2] {'ctx'}, dimensions={0}, use_global_device_ids=true | all-gather | bytes 20480 | tf_op jit(solution)/shard_map/all_gather | solution.py:111
  74.4 384.1 %while.19 = (s32[]{:T(128)}, f32[2,24,64,128]{3,2,1,0:T(8,128)}, f32[2,24,64,128]{3,2,1,0:T(8,128)S(1)}, f32[2,32,128]{2,1,0:T(8,128)}, f32[2,32,128]{2,1,0:T(8,...) while((s32[]{:T(128)}, f32[2,24,64,128]{3,2,1,0:T(8,128)}, ...), condition=%wide.region_15.16_spmd.clone, body=%wide.region_4.15_spmd.clone.sunk | while | flops 1432242560 | bytes 121302272 | solution.py:217
  98.5 2.5 fusion.104
  108.1 4.6 multiply_reduce_fusion.12
  112.7 3.5 fusion.101
  116.1 4.1 scatter_fusion
  145.6 2.5 fusion.104
  148.9 2.5 fusion.103
  156.2 4.6 multiply_reduce_fusion.12
  160.8 3.5 fusion.101
  164.3 4.1 scatter_fusion
  193.8 2.5 fusion.104
  204.4 4.6 multiply_reduce_fusion.12
  209.0 3.5 fusion.101
  212.5 4.1 scatter_fusion
  242.0 2.5 fusion.104
  245.2 2.5 fusion.103
  252.6 4.6 multiply_reduce_fusion.12
  257.2 3.5 fusion.101
  260.6 4.1 scatter_fusion
  290.1 2.5 fusion.104
  300.7 4.6 multiply_reduce_fusion.12
  305.3 3.5 fusion.101
  308.8 4.1 scatter_fusion
  338.2 2.5 fusion.104
  341.5 2.5 fusion.103
  348.8 4.6 multiply_reduce_fusion.12
  353.4 3.5 fusion.101
  356.9 4.1 scatter_fusion
  386.4 2.5 fusion.104
  397.0 4.6 multiply_reduce_fusion.12
  401.6 3.5 fusion.101
  405.1 4.1 scatter_fusion
  434.6 2.5 fusion.104
  445.1 4.6 multiply_reduce_fusion.12
  449.7 3.5 fusion.101
  453.2 4.1 scatter_fusion
  458.5 34.7 %psum.23 = f32[16,2,128]{2,1,0:T(2,128)S(1)} all-reduce(f32[16,2,128]{2,1,0:T(2,128)} %bitcast.272), channel_id=1, replica_groups=mesh['groups'=2,'ctx'=4,'dp'=2,'head'=2] {'ctx','dp'}, use_global_device_ids=true, to_apply=%region_22.23 | all-reduce | flops 4096 | bytes 32768 | tf_op jit(solution)/shard_map/psum | solution.py:263
  494.1 3.5 all-to-all-start.4
  500.5 9.2 %reduce-scatter.3.cloned.1.call-done = f32[2,8,128]{2,1,0:T(8,128)} async-done(((f32[2,32,128]{2,1,0:T(8,128)}), f32[2,8,128]{2,1,0:T(8,128)}) %reduce-scatter.3.cloned.1.call-update) | async-done | bytes 8208 | tf_op jit(solution)/shard_map/reduce_scatter | solution.py:242
  511.0 18.0 %reduce-scatter.5.cloned.1.call-done = f32[2,8,128]{2,1,0:T(8,128)} async-done(((f32[2,32,128]{2,1,0:T(8,128)}), f32[2,8,128]{2,1,0:T(8,128)}) %reduce-scatter.5.cloned.1.call-update) | async-done | bytes 8208 | tf_op jit(solution)/shard_map/reduce_scatter | solution.py:243
  532.4 3.5 all-to-all-start.3
  535.8 67.4 %all-reduce.3.cloned.1.call-done = (f32[2,64,128]{2,1,0:T(8,128)}, f32[2,64,128]{2,1,0:T(8,128)}) async-done(((f32[2,64,128]{2,1,0:T(8,128)}, f32[2,64,128]{2,1,0:T(8,128)}), (f32[2,64,128]{2,1,0:T(8,128)}, f32[2,64,128]{2,1,0:T(8,128)})) %all-reduce.3.cloned.1.call-update) | async-done | bytes 131088 | tf_op jit(solution)/shard_map/psum | solution.py:263
  (731 shorter events, 289.2 us)
Async XLA Ops:
  7.2 62.5 %copy-start.28 = (s32[1,8,2,16]{3,2,1,0:T(2,128)S(1)}, s32[1,8,2,16]{3,2,1,0:T(2,128)}, u32[]{:S(2)}) copy-start(s32[1,8,2,16]{3,2,1,0:T(2,128)} %param.14) | copy-start | bytes 3076
  7.2 44.2 %copy-start.25 = (f32[2,64,128]{2,1,0:T(8,128)S(1)}, f32[2,64,128]{2,1,0:T(8,128)}, u32[]{:S(2)}) copy-start(f32[2,64,128]{2,1,0:T(8,128)} %param.16) | copy-start | bytes 196612
  10.1 11.9 %all-to-all-start = ((s32[4,2,4]{2,1,0:T(2,128)}), s32[4,2,4]{2,1,0:T(2,128)S(1)}, u32[]{:S(2)}, u32[]{:S(2)}) async-start(s32[4,2,4]{2,1,0:T(2,128)} %copy.121), calls=%async_computation | async-start | bytes 8192 | tf_op jit(solution)/shard_map/all_to_all | solution.py:130
  17.4 55.4 %copy-start.5 = (bf16[1,512,2,128]{3,1,2,0:T(8,128)(2,1)}, bf16[1,512,2,128]{3,1,2,0:T(8,128)(2,1)S(1)}, u32[]{:S(2)}) copy-start(bf16[1,512,2,128]{3,1,2,0:T(8,128)(2,1)S(1)} %copy.170) | copy-start | bytes 786436
  23.6 24.2 %all-to-all-start.2 = ((bf16[4,2,4,64,128]{4,3,2,1,0:T(8,128)(2,1)}), bf16[4,2,4,64,128]{4,3,2,1,0:T(8,128)(2,1)S(1)}, u32[]{:S(2)}, u32[]{:S(2)}) async-start(bf16[4,2,4,64,128]{4,3,2,1,0:T(8,128)(2,1)} %bitcast.28), calls=%async_computation.2 | async-start | bytes 1048576 | tf_op jit(solution)/shard_map/all_to_all | solution.py:138
  28.1 44.7 %copy-start.7 = (bf16[1,512,2,128]{3,1,2,0:T(8,128)(2,1)}, bf16[1,512,2,128]{3,1,2,0:T(8,128)(2,1)S(1)}, u32[]{:S(2)}) copy-start(bf16[1,512,2,128]{3,1,2,0:T(8,128)(2,1)S(1)} %copy.120) | copy-start | bytes 786436
  47.8 23.6 %all-to-all-start.1 = ((bf16[4,2,4,64,128]{4,3,2,1,0:T(8,128)(2,1)}), bf16[4,2,4,64,128]{4,3,2,1,0:T(8,128)(2,1)S(1)}, u32[]{:S(2)}, u32[]{:S(2)}) async-start(bf16[4,2,4,64,128]{4,3,2,1,0:T(8,128)(2,1)} %bitcast.14), calls=%async_computation.1 | async-start | bytes 1048576 | tf_op jit(solution)/shard_map/all_to_all | solution.py:137
  51.3 458.4 %reduce-scatter.3.cloned.1.call-start = ((), (), s32[]{:S(2)}) async-start(), calls=%async_computation.7 | async-start | bytes 40960 | tf_op jit(solution)/shard_map/reduce_scatter | solution.py:242
  95.8 5.3 copy-start.13
  95.8 5.3 copy-start.20
  95.8 5.3 copy-start.30
  135.4 5.1 copy-start.12
  142.9 5.3 copy-start.13
  142.9 5.3 copy-start.20
  142.9 5.3 copy-start.30
  183.6 5.1 copy-start.12
  191.1 5.3 copy-start.13
  191.1 5.3 copy-start.20
  191.1 5.3 copy-start.30
  231.7 5.1 copy-start.12
  239.2 5.3 copy-start.13
  239.2 5.3 copy-start.20
  239.2 5.3 copy-start.30
  279.9 5.1 copy-start.12
  287.4 5.3 copy-start.13
  287.4 5.3 copy-start.20
  287.4 5.3 copy-start.30
  328.0 5.1 copy-start.12
  335.5 5.3 copy-start.13
  335.5 5.3 copy-start.20
  335.5 5.3 copy-start.30
  376.2 5.1 copy-start.12
  383.7 5.3 copy-start.13
  383.7 5.3 copy-start.20
  383.7 5.3 copy-start.30
  424.3 5.1 copy-start.12
  431.8 5.3 copy-start.13
  431.8 5.3 copy-start.20
  431.8 5.3 copy-start.30
  458.5 51.2 %copy-start.8 = (bf16[1,512,2,128]{3,1,2,0:T(8,128)(2,1)S(1)}, bf16[1,512,2,128]{3,1,2,0:T(8,128)(2,1)}, u32[]{:S(2)}) copy-start(bf16[1,512,2,128]{3,1,2,0:T(8,128)(2,1)} %copy-done.7) | copy-start | bytes 786436
  458.5 70.6 %copy-start.6 = (bf16[1,512,2,128]{3,1,2,0:T(8,128)(2,1)S(1)}, bf16[1,512,2,128]{3,1,2,0:T(8,128)(2,1)}, u32[]{:S(2)}) copy-start(bf16[1,512,2,128]{3,1,2,0:T(8,128)(2,1)} %copy-done.5) | copy-start | bytes 786436
  458.5 72.0 %copy-start.26 = (f32[2,64,128]{2,1,0:T(8,128)S(1)}, f32[2,64,128]{2,1,0:T(8,128)}, u32[]{:S(2)}) copy-start(f32[2,64,128]{2,1,0:T(8,128)} %param.16) | copy-start | bytes 196612
  458.5 72.8 %copy-start.27 = (f32[2,64,128]{2,1,0:T(8,128)S(1)}, f32[2,64,128]{2,1,0:T(8,128)}, u32[]{:S(2)}) copy-start(f32[2,64,128]{2,1,0:T(8,128)} %param.15) | copy-start | bytes 196612
  494.1 38.2 %all-to-all-start.4 = ((bf16[4,2,4,64,128]{4,3,2,1,0:T(8,128)(2,1)}), bf16[4,2,4,64,128]{4,3,2,1,0:T(8,128)(2,1)S(1)}, u32[]{:S(2)}, u32[]{:S(2)}) async-start(bf16[4,2,4,64,128]{4,3,2,1,0:T(8,128)(2,1)} %copy.129), calls=%async_computation.6 | async-start | bytes 1048576 | tf_op jit(solution)/shard_map/all_to_all | solution.py:235
  497.6 108.8 %copy-start.15 = (s32[32]{0:T(128)S(1)}, s32[32]{0:T(128)}, u32[]{:S(2)}) copy-start(s32[32]{0:T(128)} %reshape.254) | copy-start | bytes 388
  497.6 31.4 %reduce-scatter.5.cloned.1.call-start = ((), (), s32[]{:S(2)}) async-start(), calls=%async_computation.8 | async-start | bytes 40960 | tf_op jit(solution)/shard_map/reduce_scatter | solution.py:243
  500.4 102.8 %all-reduce.3.cloned.1.call-start = ((), (), s32[]{:S(2)}) async-start(), calls=%async_computation.9 | async-start | bytes 262144 | tf_op jit(solution)/shard_map/psum | solution.py:263
  532.4 77.4 %all-to-all-start.3 = ((bf16[4,2,4,64,128]{4,3,2,1,0:T(8,128)(2,1)}), bf16[4,2,4,64,128]{4,3,2,1,0:T(8,128)(2,1)S(1)}, u32[]{:S(2)}, u32[]{:S(2)}) async-start(bf16[4,2,4,64,128]{4,3,2,1,0:T(8,128)(2,1)} %copy.127), calls=%async_computation.4 | async-start | bytes 1048576 | tf_op jit(solution)/shard_map/all_to_all | solution.py:232
  (153 other events, 473.6 us)
Sparse Core Ops, SparseCore 0:
  493.3 16.2 reduce-scatter.2
  512.0 17.0 reduce-scatter.4
  533.1 70.1 all-reduce.2
where the time goes:
time: 624 us; the launch traced here: 620 us
  matrix products  204 us (33%)
  local copies, waits for them, and re-layouts  107 us (17%)
  other arithmetic  103 us (17%)
  waiting for transfers between devices  99.2 us (16%)
  blocking collectives  69.6 us (11%)
  starting transfers between devices  20.3 us (3%)
  between operations  14 us (2%)
    psum x1, waiting for transfers between devices, on_device(): lax.psum((weight_key, weight_value, gate_acc.reshape(kv_heads * group, 2,...  67.4 us
    dot_general x16, matrix products, branch_grads(): jnp.einsum('gtnk,tgnd->gkd', score_grad, queried, preferred_element_type=...  46.8 us
    dot_general x16, matrix products, branch_grads(): jnp.einsum('tgnd,gkd->gtnk', back_rounded, piece_values, preferred_elemen...  41.9 us
    dot_general x16, matrix products, branch_grads(): jnp.einsum('gtnk,tgnd->gkd', rounded, back_rounded, preferred_element_typ...  38.7 us
    psum x1, blocking collectives, on_device(): lax.psum((weight_key, weight_value, gate_acc.reshape(kv_heads * group, 2,...  34.7 us
    scatter-add x8, other arithmetic, advance(): key_acc.at[head_range, lookup]  32.6 us
    dynamic_slice x16, local copies, waits for them, and re-layouts, on_device(): lax.scan(advance, start, (query_blocks, teacher_blocks, chosen_all, looku...  24.2 us
    scatter-add x8, other arithmetic, advance(): value_acc.at[head_range, lookup]  19.4 us
  transfers between devices with their start and end apart: 8, of which 4 were waited for; matrix products, arithmetic and copies ran while one was open for 3% of the time, Pallas kernels for 0%

commit v1 on v0

v1 whole, which is shorter than its diff:
```python
import functools
import math

import jax
import jax.numpy as jnp
from jax import lax
from jax.experimental import pallas as pl
from jax.experimental.pallas import tpu as pltpu
from jax.sharding import PartitionSpec as P

HIGHEST = lax.Precision.HIGHEST
MASKED = -1e30
NT = (((1,), (1,)), ((), ()))
NN = (((1,), (0,)), ((), ()))
TN = (((0,), (0,)), ((), ()))


def dot(a, b, dims):
    return lax.dot_general(a, b, dims, preferred_element_type=jnp.float32)


def fold(x, op):
    return op(x.reshape(x.shape[0] // 8, 8, x.shape[1]), axis=0)


def attend_kernel(
    dims,
    bias_ref,
    q_ref,
    t_ref,
    k_ref,
    v_ref,
    ck_ref,
    cv_ref,
    gw_ref,
    cur_ref,
    dk_ref,
    dv_ref,
    dck_ref,
    dcv_ref,
    dgw_ref,
    s_scr,
    d_scr,
    vt_scr,
    ot_scr,
    tri_scr,
):
    kv_heads, group, span, remote_slots, own_blocks, chunk_slots, pair = dims
    slots = remote_slots + own_blocks
    chunk = chunk_slots * span
    head_dim = q_ref.shape[-1]
    rows = span * group
    factor = head_dim ** (-0.5)
    power = factor * math.log2(math.e)
    j = pl.program_id(0)
    chunks = (remote_slots + j) // chunk_slots + 1

    @pl.when(j == 0)
    def _():
        dk_ref[...] = jnp.zeros_like(dk_ref)
        dv_ref[...] = jnp.zeros_like(dv_ref)
        dck_ref[...] = jnp.zeros_like(dck_ref)
        dcv_ref[...] = jnp.zeros_like(dcv_ref)
        dgw_ref[...] = jnp.zeros_like(dgw_ref)
        key_at = lax.broadcasted_iota(jnp.int32, (span, rows), 0)
        row_at = lax.broadcasted_iota(jnp.int32, (span, rows), 1) // group
        tri_scr[...] = jnp.where(key_at <= row_at, 0.0, MASKED)

        def turn(c, _):
            at = pl.ds(pl.multiple_of(c * chunk, chunk), chunk)
            for g in range(kv_heads):
                vt_scr[g, :, at] = v_ref[g, at, :].astype(jnp.float32).T.astype(jnp.bfloat16)
            return 0

        lax.fori_loop(0, slots // chunk_slots, turn, 0)

    for base in range(0, kv_heads, pair):
        heads = [(p, base + p) for p in range(pair)]
        wide = {}
        narrow = {}
        for p, g in heads:
            wide[p] = (
                q_ref[...].astype(jnp.float32)[:, g * group : (g + 1) * group, :]
            )
            narrow[p] = wide[p].reshape(rows, head_dim).astype(jnp.bfloat16)

        def scores(c, peaks):
            at = pl.ds(pl.multiple_of(c * chunk, chunk), chunk)
            out = []
            for p, g in heads:
                s = dot(k_ref[g, at, :], narrow[p], NT)
                parts = []
                for i in range(chunk_slots):
                    b = bias_ref[(j * kv_heads + g) * slots + c * chunk_slots + i]
                    parts.append(s[i * span : (i + 1) * span] + b)
                s = jnp.concatenate(parts, axis=0)
                s_scr[p, at, :] = s
                out.append(jnp.maximum(peaks[p], fold(s, jnp.max)))
            return tuple(out)

        peaks = lax.fori_loop(
            0, chunks, scores, tuple(jnp.full((8, rows), MASKED, jnp.float32) for _ in heads)
        )
        own = pl.ds(pl.multiple_of((remote_slots + j) * span, span), span)
        peak = {}
        for p, g in heads:
            s = dot(k_ref[g, own, :], narrow[p], NT) + tri_scr[...]
            s_scr[p, own, :] = s
            peak[p] = jnp.max(
                jnp.maximum(peaks[p], fold(s, jnp.max)), axis=0, keepdims=True
            )

        def raise_all(c, sums):
            at = pl.ds(pl.multiple_of(c * chunk, chunk), chunk)
            out = []
            for p, g in heads:
                e = jnp.exp2((s_scr[p, at, :] - peak[p]) * power)
                s_scr[p, at, :] = e
                out.append(sums[p] + fold(e, jnp.sum))
            return tuple(out)

        sums = lax.fori_loop(
            0, chunks, raise_all, tuple(jnp.zeros((8, rows), jnp.float32) for _ in heads)
        )
        inverse = {p: 1.0 / jnp.sum(sums[p], axis=0, keepdims=True) for p, g in heads}
        ot_scr[...] = jnp.zeros_like(ot_scr)

        def outputs(c, _):
            at = pl.ds(pl.multiple_of(c * chunk, chunk), chunk)
            for p, g in heads:
                w = s_scr[p, at, :] * inverse[p]
                s_scr[p, at, :] = w
                ot_scr[p] += dot(vt_scr[g, :, at], w.astype(jnp.bfloat16), NN)
            return 0

        lax.fori_loop(0, chunks, outputs, 0)

        backs = {}
        for p, g in heads:
            sel_out = ot_scr[p].T
            ck = ck_ref[g]
            cv = cv_ref[g]
            cs = dot(ck, narrow[p], NT)
            at_block = lax.broadcasted_iota(jnp.int32, cs.shape, 0)
            usable = at_block <= cur_ref[0] + j
            cs = jnp.where(usable, cs, MASKED)
            ce = jnp.exp2((cs - jnp.max(cs, axis=0, keepdims=True)) * power)
            cw = ce * (1.0 / jnp.sum(ce, axis=0, keepdims=True))
            cr = cw.astype(jnp.bfloat16)
            comp_out = dot(cv, cr, TN).T
            q3 = wide[p]
            gates = []
            for r in range(2):
                logit = jnp.sum(q3 * gw_ref[g, r][None], axis=-1, keepdims=True)
                gates.append(jax.nn.sigmoid(logit))
            comp3 = comp_out.reshape(span, group, head_dim)
            sel3 = sel_out.reshape(span, group, head_dim)
            t3 = t_ref[...].astype(jnp.float32)[:, g * group : (g + 1) * group, :]
            error = gates[0] * comp3 + gates[1] * sel3 - t3
            for r, branch in ((0, comp3), (1, sel3)):
                term = jnp.sum(error * branch, axis=-1, keepdims=True) * (
                    gates[r] * (1.0 - gates[r])
                )
                dgw_ref[g, r] += jnp.sum(term * q3, axis=0)
            backs[p] = (gates[1] * error).reshape(rows, head_dim).astype(jnp.bfloat16)
            cb = (gates[0] * error).reshape(rows, head_dim).astype(jnp.bfloat16)
            cd = dot(cv, cb, NT)
            total = jnp.sum(cw * cd, axis=0, keepdims=True)
            cg = (factor * cw * (cd - total)).astype(jnp.bfloat16)
            dck_ref[g] += dot(cg, narrow[p], NN)
            dcv_ref[g] += dot(cr, cb, NN)

        def weight_grads(c, totals):
            at = pl.ds(pl.multiple_of(c * chunk, chunk), chunk)
            out = []
            for p, g in heads:
                d = dot(v_ref[g, at, :], backs[p], NT)
                d_scr[p, at, :] = d
                out.append(totals[p] + fold(s_scr[p, at, :] * d, jnp.sum))
            return tuple(out)

        totals = lax.fori_loop(
            0, chunks, weight_grads, tuple(jnp.zeros((8, rows), jnp.float32) for _ in heads)
        )
        total = {p: jnp.sum(totals[p], axis=0, keepdims=True) for p, g in heads}

        def key_grads(c, _):
            at = pl.ds(pl.multiple_of(c * chunk, chunk), chunk)
            for p, g in heads:
                w = s_scr[p, at, :]
                sg = (w * ((d_scr[p, at, :] - total[p]) * factor)).astype(jnp.bfloat16)
                dk_ref[g, at, :] += dot(sg, narrow[p], NN)
                dv_ref[g, at, :] += dot(w.astype(jnp.bfloat16), backs[p], NN)
            return 0

        lax.fori_loop(0, chunks, key_grads, 0)


def attend(queries, teacher, keys, values, comp_keys, comp_values, gate_pairs, bias, first, dims):
    kv_heads, group, span, remote_slots, own_blocks, chunk_slots, pair = dims
    slots = remote_slots + own_blocks
    head_dim = keys.shape[-1]
    all_blocks = comp_keys.shape[1]
    rows = span * group
    whole = pl.BlockSpec(memory_space=pltpu.VMEM)
    scalars = pl.BlockSpec(memory_space=pltpu.SMEM)
    tokens = pl.BlockSpec((span, kv_heads * group, head_dim), lambda j: (j, 0, 0))
    f32 = jnp.float32
    flops = own_blocks * kv_heads * rows * slots * span * head_dim * 10
    return pl.pallas_call(
        functools.partial(attend_kernel, dims),
        grid=(own_blocks,),
        in_specs=[scalars, tokens, tokens, whole, whole, whole, whole, whole, scalars],
        out_specs=[whole] * 5,
        out_shape=[
            jax.ShapeDtypeStruct((kv_heads, slots * span, head_dim), f32),
            jax.ShapeDtypeStruct((kv_heads, slots * span, head_dim), f32),
            jax.ShapeDtypeStruct((kv_heads, all_blocks, head_dim), f32),
            jax.ShapeDtypeStruct((kv_heads, all_blocks, head_dim), f32),
            jax.ShapeDtypeStruct((kv_heads, 2, group, head_dim), f32),
        ],
        scratch_shapes=[
            pltpu.VMEM((pair, slots * span, rows), f32),
            pltpu.VMEM((pair, slots * span, rows), f32),
            pltpu.VMEM((kv_heads, head_dim, slots * span), jnp.bfloat16),
            pltpu.VMEM((pair, head_dim, rows), f32),
            pltpu.VMEM((span, rows), f32),
        ],
        compiler_params=pltpu.CompilerParams(vmem_limit_bytes=60 * 1024 * 1024),
        cost_estimate=pl.CostEstimate(flops=flops, bytes_accessed=8 << 20, transcendentals=0),
    )(bias, queries, teacher, keys, values, comp_keys, comp_values, gate_pairs, first)


def on_device(
    queries,
    key_states,
    value_states,
    teacher_out,
    selection,
    compress_keys,
    compress_values,
    gate_weights,
):
    ctx_count = lax.axis_size("ctx")
    my_index = lax.axis_index("ctx")
    tokens_dev = key_states.shape[1]
    kv_heads = key_states.shape[2]
    head_dim = key_states.shape[3]
    span = compress_keys.shape[1]
    own_blocks = tokens_dev // span
    all_blocks = own_blocks * ctx_count
    group = queries.shape[2] // kv_heads
    key_blocks = key_states[0].reshape(own_blocks, span, kv_heads, head_dim)
    value_blocks = value_states[0].reshape(own_blocks, span, kv_heads, head_dim)
    comp_local = jnp.stack(
        [
            jnp.sum(key_blocks.astype(jnp.float32) * compress_keys.transpose(1, 0, 2)[None], axis=1),
            jnp.sum(
                value_blocks.astype(jnp.float32) * compress_values.transpose(1, 0, 2)[None], axis=1
            ),
        ]
    ).astype(jnp.bfloat16)
    comp_all = lax.all_gather(comp_local, "ctx", axis=1, tiled=True).transpose(0, 2, 1, 3)
    comp_keys, comp_values = comp_all[0], comp_all[1]
    chosen = selection[0]
    pieces = jnp.stack(
        [key_blocks.transpose(2, 0, 1, 3), value_blocks.transpose(2, 0, 1, 3)], axis=2
    )
    capacity = own_blocks // 2
    hits = jnp.any(chosen[..., None] == jnp.arange(all_blocks), axis=2)
    hits = hits.astype(jnp.int32).reshape(own_blocks, kv_heads, ctx_count, own_blocks)
    present = jnp.max(hits, axis=0)
    earlier = jnp.arange(own_blocks)[:, None] < jnp.arange(own_blocks)[None, :]
    slot_rank = jnp.sum(present[..., :, None] * earlier.astype(jnp.int32), axis=-2)
    slot_hit = (
        (present[..., None] == 1) & (slot_rank[..., None] == jnp.arange(capacity))
    ).astype(jnp.int32)
    request = jnp.sum(slot_hit * jnp.arange(own_blocks)[:, None], axis=2)
    asked = lax.all_to_all(
        request.transpose(1, 0, 2), "ctx", split_axis=0, concat_axis=0, tiled=True
    )
    head_pick = jnp.arange(kv_heads)[None, :, None]
    send = pieces[head_pick, asked]
    got = lax.all_to_all(send, "ctx", split_axis=0, concat_axis=0, tiled=True)
    others = (my_index + 1 + jnp.arange(ctx_count - 1)) % ctx_count
    got = got[others]
    remote_slots = (ctx_count - 1) * capacity
    slots = remote_slots + own_blocks
    got = got.transpose(3, 1, 0, 2, 4, 5).reshape(2, kv_heads, remote_slots * span, head_dim)
    local = pieces.transpose(2, 0, 1, 3, 4).reshape(2, kv_heads, tokens_dev, head_dim)
    both = jnp.concatenate([got, local], axis=2)
    slot_on = jnp.einsum("jhob,hobc->jhoc", hits, slot_hit)[:, :, others].reshape(
        own_blocks, kv_heads, remote_slots
    )
    local_on = lax.dynamic_index_in_dim(hits, my_index, axis=2, keepdims=False)
    below = jnp.arange(own_blocks)[None, :] < jnp.arange(own_blocks)[:, None]
    local_on = local_on * below.astype(jnp.int32)[:, None, :]
    bias = jnp.where(jnp.concatenate([slot_on, local_on], axis=-1) > 0, 0.0, MASKED)
    bias = bias.astype(jnp.float32).reshape(-1)
    dims = (
        kv_heads,
        group,
        span,
        remote_slots,
        own_blocks,
        capacity,
        kv_heads if slots <= 40 else 1,
    )
    gate_pairs = gate_weights.reshape(kv_heads, group, 2, head_dim).transpose(0, 2, 1, 3)
    first = (my_index * own_blocks).astype(jnp.int32).reshape(1)
    key_acc, value_acc, comp_key_acc, comp_value_acc, gate_acc = attend(
        queries[0],
        teacher_out[0],
        both[0],
        both[1],
        comp_keys,
        comp_values,
        gate_pairs,
        bias,
        first,
        dims,
    )
    accs = jnp.stack([key_acc, value_acc]).reshape(2, kv_heads, slots, span, head_dim)
    back = accs[:, :, :remote_slots].reshape(
        2, kv_heads, ctx_count - 1, capacity, span, head_dim
    ).transpose(2, 1, 3, 0, 4, 5)
    back = jnp.concatenate([back, jnp.zeros_like(back[:1])], axis=0)
    back = back[(jnp.arange(ctx_count) - my_index - 1) % ctx_count].astype(jnp.bfloat16)
    returned = lax.all_to_all(back, "ctx", split_axis=0, concat_axis=0, tiled=True)
    place = (asked[..., None] == jnp.arange(own_blocks)).astype(jnp.bfloat16)
    added = jnp.einsum(
        "ohcb,ohcrud->rhbud", place, returned, preferred_element_type=jnp.float32
    )
    piece_grad = accs[:, :, remote_slots:] + added
    comp_own = lax.psum_scatter(
        jnp.stack([comp_key_acc, comp_value_acc]), "ctx", scatter_dimension=2, tiled=True
    )
    compress = jnp.stack([compress_keys, compress_values])
    totals = piece_grad + compress[:, :, None, :, :] * comp_own[:, :, :, None, :]
    grads = (
        totals.transpose(0, 2, 3, 1, 4)
        .reshape(2, tokens_dev, kv_heads, head_dim)
        .astype(jnp.bfloat16)
    )
    weight_grads = jnp.sum(
        comp_own[:, :, :, None, :] * local.reshape(piece_grad.shape).astype(jnp.float32), axis=2
    )
    gate_part = gate_acc.transpose(0, 2, 1, 3).reshape(kv_heads * group, 2, head_dim)
    summed = lax.psum((weight_grads, gate_part), ("ctx", "dp"))
    divisor = math.sqrt(lax.axis_size("dp") * ctx_count * tokens_dev)
    return (
        grads[0][None],
        grads[1][None],
        summed[0][0] / divisor,
        summed[0][1] / divisor,
        summed[1] / divisor,
    )


def solution(mesh):
    tokens = P(("groups", "dp"), "ctx", "head", None)
    weights = P("head", None, None)
    sums = P(("groups", "head"), None, None)
    return jax.shard_map(
        on_device,
        mesh=mesh,
        in_specs=(tokens,) * 5 + (weights,) * 3,
        out_specs=(tokens, tokens, sums, sums, sums),
        check_vma=False,
    )
```

time: 624 us -> 277 us (0.44)
  matrix products: 204 us -> 3.04 us
  other arithmetic: 103 us -> 8.85 us
  local copies, waits for them, and re-layouts: 107 us -> 25.4 us
  Pallas kernels: 0 us -> 71.4 us
  waiting for transfers between devices: 99.2 us -> 66 us
    dot_general x96 -> x2, matrix products: 204 us -> 3.04 us  [the longest x1 2.9 us: on_device(): jnp.einsum('ohcb,ohcrud->rhbud', place, returned, preferred_element_type=...]
    pallas_call x0 -> x1, Pallas kernels: none -> 71.4 us  [attend(): pl.pallas_call(functools.partial(attend_kernel, dims), grid=(own_blocks,)...]
    scatter-add x18 -> x0, other arithmetic: 56.7 us -> none  [the longest x8 32.6 us: advance(): key_acc.at[head_range, lookup]]
    reduce_scatter x2 -> x1, waiting for transfers between devices: 27.2 us -> 0.01 us  [on_device(): lax.psum_scatter(jnp.stack([comp_key_acc, comp_value_acc]), 'ctx', scatte...]
    gather x18 -> x5, local copies, waits for them, and re-layouts: 31.9 us -> 5.84 us  [the longest x1 2.89 us: on_device(): back[(jnp.arange(ctx_count) - my_index - 1) % ctx_count]]
    dynamic_slice x16 -> x0, local copies, waits for them, and re-layouts: 24.2 us -> none  [on_device(): lax.scan(advance, start, (query_blocks, teacher_blocks, chosen_all, looku...]
    while x368 -> x0, local copies, waits for them, and re-layouts: 15 us -> none
    reduce_sum x18 -> x5, other arithmetic: 15 us -> 2.9 us  [the longest x1 2.43 us: on_device(): jnp.sum(comp_own[:, :, :, None, :] * local.reshape(piece_grad.shape).asty...]
  transfers between devices with their start and end apart: 8 -> 5, of which waited for: 4 -> 2; matrix products, arithmetic and copies ran while one was open for 3% -> 6% of each run, Pallas kernels for 0% -> 0%
where the time goes in v1:
time: 277 us; the launch traced here: 276 us
  blocking collectives  73 us (26%)
  Pallas kernels  71.4 us (26%)
  waiting for transfers between devices  66 us (24%)
  local copies, waits for them, and re-layouts  25.4 us (9%)
  starting transfers between devices  14.3 us (5%)
  between operations  14.3 us (5%)
  other arithmetic  8.85 us (3%)
  matrix products  3.04 us (1%)
    pallas_call x1, Pallas kernels, attend(): pl.pallas_call(functools.partial(attend_kernel, dims), grid=(own_blocks,)...  71.4 us
    psum x1, waiting for transfers between devices, on_device(): summed = lax.psum((weight_grads, gate_part), ('ctx', 'dp'))  64 us
    psum x1, blocking collectives, on_device(): summed = lax.psum((weight_grads, gate_part), ('ctx', 'dp'))  45.3 us
    all_gather x1, blocking collectives, on_device(): lax.all_gather(comp_local, 'ctx', axis=1, tiled=True).transpose(0, 2, 1, 3)  27.7 us
    unnamed x19, local copies, waits for them, and re-layouts  8 us
    all_to_all x1, starting transfers between devices, on_device(): lax.all_to_all(request.transpose(1, 0, 2), 'ctx', split_axis=0, concat_ax...  6.32 us
  transfers between devices with their start and end apart: 5, of which 2 were waited for; matrix products, arithmetic and copies ran while one was open for 6% of the time, Pallas kernels for 0%

profile of v1, /device:TPU:0, one launch (start us, length us, event | category | flops | bytes accessed | tf_op | source)
XLA Modules:
  0.0 276.3 jit_solution(4664990947246106291)
XLA Ops:
  7.2 0.8 fusion.6
  8.1 0.1 multiply_reduce_fusion.3
  8.2 0.2 select_reduce_fusion
  8.4 0.6 copy.139
  9.0 6.3 %all-to-all-start = ((s32[4,2,4]{2,1,0:T(2,128)}), s32[4,2,4]{2,1,0:T(2,128)S(1)}, u32[]{:S(2)}, u32[]{:S(2)}) async-start(s32[4,2,4]{2,1,0:T(2,128)} %copy.139), calls=%async_computation | async-start | bytes 8192 | tf_op jit(solution)/shard_map/all_to_all | solution.py:279
  15.4 1.0 copy.137
  16.4 1.0 copy.135
  17.3 0.3 copy_bitcast_fusion.1
  17.7 0.1 fusion.29
  17.8 0.6 copy-done
  18.4 0.2 copy.140
  18.6 0.2 copy.142
  18.9 2.0 all-to-all-done
  20.9 0.1 reshape.225
  21.0 1.7 gather_fusion.1
  22.7 3.7 %all-to-all-start.1 = ((bf16[4,2,4,2,64,128]{5,4,3,2,1,0:T(8,128)(2,1)}), bf16[4,2,4,2,64,128]{5,4,3,2,1,0:T(8,128)(2,1)S(1)}, u32[]{:S(2)}, u32[]{:S(2)}) async-start(bf16[4,2,4,2,64,128]{5,4,3,2,1,0:T(8,128)(2,1)} %bitcast.16), calls=%async_computation.1 | async-start | bytes 2097152 | tf_op jit(solution)/shard_map/all_to_all | solution.py:284
  26.4 0.1 convolution_bitcast_fusion
  26.5 0.6 gather_fusion
  27.1 0.1 copy.133
  27.3 0.7 select_n.68.bias_ref
  28.0 0.6 copy.181
  28.8 27.7 %all_gather.3 = bf16[2,32,2,128]{3,1,2,0:T(8,128)(2,1)S(1)} all-gather(bf16[2,8,2,128]{3,1,2,0:T(8,128)(2,1)S(1)} %pad_maximum_fusion.4), channel_id=1, replica_groups=mesh['groups'=2,'ctx'=4,'dp'=2,'head'=2] {'ctx'}, dimensions={1}, use_global_device_ids=true | all-gather | bytes 40960 | tf_op jit(solution)/shard_map/all_gather | solution.py:263
  56.5 0.6 slice_bitcast_fusion
  57.1 0.7 gather_fusion.2
  57.9 1.2 fusion.4
  59.1 71.4 %shard_map.119 = (f32[2,1280,128]{2,1,0:T(8,128)}, f32[2,1280,128]{2,1,0:T(8,128)}, f32[2,32,128]{2,1,0:T(8,128)}, f32[2,32,128]{2,1,0:T(8,128)}, f32[2,2,8,128]{3,2,1,0:T(8,128)}) custom-call(f32[320]{0:T(512)} %select_n.68.bias_ref, bf16[512,16,128]{2,1,0:T(8,128)(2,1)} %bitcast.124, bf16[512,16,128]{2,1,0:T(8,128)(2,1)} %bitcast.125, ...), custom_call_target="tpu_custom_call" | custom-call | flops 13421772800 | bytes 8388608 | tf_op jit(solution)/shard_map/pallas_call | solution.py:210
  130.5 2.2 copy_dynamic-update-slice_fusion.1
  132.8 0.8 copy_dynamic-update-slice_fusion
  133.5 0.2 slice.61
  133.7 0.5 copy.147
  134.3 1.2 concatenate.16
  135.5 2.9 %gather_fusion.3 = bf16[4,2,4,2,64,128]{5,4,3,2,1,0:T(8,128)(2,1)} fusion(bf16[4,2,4,2,64,128]{5,4,3,2,1,0:T(8,128)(2,1)} %concatenate.16, s32[1024]{0:T(1024)S(1)} %pad_clamp_fusion), kind=kCustom, calls=%fused_computation.3 | custom fusion | bytes 2097168 | tf_op jit(solution)/shard_map/gather | solution.py:328
  138.4 3.1 %copy.149 = bf16[4,2,4,2,64,128]{5,2,4,3,1,0:T(4,128)(2,1)} copy(bf16[4,2,4,2,64,128]{5,4,3,2,1,0:T(8,128)(2,1)} %gather_fusion.3) | data formatting | bytes 2097152 | tf_op jit(solution)/shard_map/convert_element_type | solution.py:328
  141.5 4.2 %all-to-all-start.2 = ((bf16[4,2,4,2,64,128]{5,2,4,3,1,0:T(4,128)(2,1)}), bf16[4,2,4,2,64,128]{5,2,4,3,1,0:T(4,128)(2,1)}, u32[]{:S(2)}, u32[]{:S(2)}) async-start(bf16[4,2,4,2,64,128]{5,2,4,3,1,0:T(4,128)(2,1)} %copy.149), calls=%async_computation.2 | async-start | bytes 2097152 | tf_op jit(solution)/shard_map/all_to_all | solution.py:329
  145.9 0.1 copy.151
  146.0 1.4 pad_maximum_fusion.3
  147.4 0.7 copy_bitcast_fusion.4
  148.2 45.3 %psum.15 = f32[16,2,128]{2,0,1:T(8,128)} all-reduce(f32[16,2,128]{2,0,1:T(8,128)S(1)} %copy_bitcast_fusion.4), channel_id=1, replica_groups=mesh['groups'=2,'ctx'=4,'dp'=2,'head'=2] {'ctx','dp'}, use_global_device_ids=true, to_apply=%region_9.10 | all-reduce | flops 4096 | bytes 32768 | tf_op jit(solution)/shard_map/psum | solution.py:349
  193.4 0.7 broadcast_multiply_fusion
  194.2 0.6 copy.159
  194.8 2.9 %fusion.12 = f32[2,2,64,128,8,1]{3,4,2,1,0,5:T(8,128)} fusion(bf16[4,2,4,2,64,128]{5,2,4,3,1,0:T(4,128)(2,1)} %all-to-all-done.2, s32[4,2,4]{2,1,0:T(2,128)} %copy-done.5), kind=kOutput, calls=%fused_computation.44 | convolution fusion | flops 8388864 | bytes 2097280 | tf_op jit(solution)/shard_map/ohcb,ohcrud->rhbud/dot_general | solution.py:331
  197.7 2.4 multiply_reduce_fusion
  200.1 0.6 copy.165
  200.8 1.1 fusion.30
  201.9 1.0 copy.157
  203.0 1.0 copy.158
  203.9 64.0 %all-reduce.3.cloned.1.call-done = f32[2,2,64,128]{3,2,0,1:T(8,128)} async-done(((f32[2,2,64,128]{3,2,0,1:T(8,128)}), f32[2,2,64,128]{3,2,0,1:T(8,128)}) %all-reduce.3.cloned.1.call-update) | async-done | bytes 131088 | tf_op jit(solution)/shard_map/psum | solution.py:349
  267.9 1.5 fusion.7
  (43 shorter events, 0.9 us)
Async XLA Ops:
  9.0 11.9 %all-to-all-start = ((s32[4,2,4]{2,1,0:T(2,128)}), s32[4,2,4]{2,1,0:T(2,128)S(1)}, u32[]{:S(2)}, u32[]{:S(2)}) async-start(s32[4,2,4]{2,1,0:T(2,128)} %copy.139), calls=%async_computation | async-start | bytes 8192 | tf_op jit(solution)/shard_map/all_to_all | solution.py:279
  17.7 0.7 copy-start
  20.9 1.8 copy-start.5
  22.7 5.3 %copy-start.4 = (f32[16,2,128]{2,1,0:T(2,128)S(1)}, f32[16,2,128]{2,1,0:T(2,128)}, u32[]{:S(2)}) copy-start(f32[16,2,128]{2,1,0:T(2,128)} %param.15) | copy-start | bytes 49156
  22.7 5.9 %copy-start.2 = (f32[2,64,128]{2,1,0:T(8,128)S(1)}, f32[2,64,128]{2,1,0:T(8,128)}, u32[]{:S(2)}) copy-start(f32[2,64,128]{2,1,0:T(8,128)} %param.14) | copy-start | bytes 196612
  22.7 6.0 %copy-start.3 = (f32[2,64,128]{2,1,0:T(8,128)S(1)}, f32[2,64,128]{2,1,0:T(8,128)}, u32[]{:S(2)}) copy-start(f32[2,64,128]{2,1,0:T(8,128)} %param.13) | copy-start | bytes 196612
  22.7 34.4 %all-to-all-start.1 = ((bf16[4,2,4,2,64,128]{5,4,3,2,1,0:T(8,128)(2,1)}), bf16[4,2,4,2,64,128]{5,4,3,2,1,0:T(8,128)(2,1)S(1)}, u32[]{:S(2)}, u32[]{:S(2)}) async-start(bf16[4,2,4,2,64,128]{5,4,3,2,1,0:T(8,128)(2,1)} %bitcast.16), calls=%async_computation.1 | async-start | bytes 2097152 | tf_op jit(solution)/shard_map/all_to_all | solution.py:284
  130.5 2.2 copy-start.1
  141.5 53.2 %all-to-all-start.2 = ((bf16[4,2,4,2,64,128]{5,2,4,3,1,0:T(4,128)(2,1)}), bf16[4,2,4,2,64,128]{5,2,4,3,1,0:T(4,128)(2,1)}, u32[]{:S(2)}, u32[]{:S(2)}) async-start(bf16[4,2,4,2,64,128]{5,2,4,3,1,0:T(4,128)(2,1)} %copy.149), calls=%async_computation.2 | async-start | bytes 2097152 | tf_op jit(solution)/shard_map/all_to_all | solution.py:329
  145.8 51.9 %reduce-scatter.2.cloned.1.call-start = ((), (), s32[]{:S(2)}) async-start(), calls=%async_computation.4 | async-start | bytes 81920 | tf_op jit(solution)/shard_map/reduce_scatter | solution.py:335
  147.4 120.5 %all-reduce.3.cloned.1.call-start = ((), (), s32[]{:S(2)}) async-start(), calls=%async_computation.5 | async-start | bytes 262144 | tf_op jit(solution)/shard_map/psum | solution.py:349
Sparse Core Ops, SparseCore 0:
  149.4 20.7 reduce-scatter.1
  200.9 66.9 all-reduce.2

commit v2 on v1

--- a/solution.py
+++ b/solution.py
@@ -231,6 +231,17 @@
     )(bias, queries, teacher, keys, values, comp_keys, comp_values, gate_pairs, first)
 
 
+def sum_everywhere(rows, axes):
+    count = math.prod(lax.axis_size(axis) for axis in axes)
+    total, lanes = rows.shape
+    share = -(-total // (8 * count)) * 8
+    padded = jnp.pad(rows, ((0, share * count - total), (0, 0))).reshape(count, share, lanes)
+    parts = lax.all_to_all(padded, axes, split_axis=0, concat_axis=0, tiled=True)
+    mine = jnp.broadcast_to(jnp.sum(parts, axis=0)[None], parts.shape)
+    every = lax.all_to_all(mine, axes, split_axis=0, concat_axis=0, tiled=True)
+    return every.reshape(share * count, lanes)[:total]
+
+
 def on_device(
     queries,
     key_states,
@@ -260,8 +271,6 @@
             ),
         ]
     ).astype(jnp.bfloat16)
-    comp_all = lax.all_gather(comp_local, "ctx", axis=1, tiled=True).transpose(0, 2, 1, 3)
-    comp_keys, comp_values = comp_all[0], comp_all[1]
     chosen = selection[0]
     pieces = jnp.stack(
         [key_blocks.transpose(2, 0, 1, 3), value_blocks.transpose(2, 0, 1, 3)], axis=2
@@ -280,8 +289,16 @@
         request.transpose(1, 0, 2), "ctx", split_axis=0, concat_axis=0, tiled=True
     )
     head_pick = jnp.arange(kv_heads)[None, :, None]
-    send = pieces[head_pick, asked]
-    got = lax.all_to_all(send, "ctx", split_axis=0, concat_axis=0, tiled=True)
+    send = pieces[head_pick, asked].reshape(ctx_count, -1, head_dim)
+    comp_rows = comp_local.transpose(0, 2, 1, 3).reshape(-1, head_dim)
+    comp_send = jnp.broadcast_to(comp_rows[None], (ctx_count,) + comp_rows.shape)
+    mixed = lax.all_to_all(
+        jnp.concatenate([send, comp_send], axis=1), "ctx", split_axis=0, concat_axis=0, tiled=True
+    )
+    got = mixed[:, : send.shape[1]].reshape(ctx_count, kv_heads, capacity, 2, span, head_dim)
+    comp_all = mixed[:, send.shape[1] :].reshape(ctx_count, 2, kv_heads, own_blocks, head_dim)
+    comp_all = comp_all.transpose(1, 2, 0, 3, 4).reshape(2, kv_heads, all_blocks, head_dim)
+    comp_keys, comp_values = comp_all[0], comp_all[1]
     others = (my_index + 1 + jnp.arange(ctx_count - 1)) % ctx_count
     got = got[others]
     remote_slots = (ctx_count - 1) * capacity
@@ -332,8 +349,14 @@
         "ohcb,ohcrud->rhbud", place, returned, preferred_element_type=jnp.float32
     )
     piece_grad = accs[:, :, remote_slots:] + added
-    comp_own = lax.psum_scatter(
-        jnp.stack([comp_key_acc, comp_value_acc]), "ctx", scatter_dimension=2, tiled=True
+    comp_parts = jnp.stack([comp_key_acc, comp_value_acc]).reshape(
+        2, kv_heads, ctx_count, own_blocks, head_dim
+    )
+    comp_own = jnp.sum(
+        lax.all_to_all(
+            comp_parts.transpose(2, 0, 1, 3, 4), "ctx", split_axis=0, concat_axis=0, tiled=True
+        ),
+        axis=0,
     )
     compress = jnp.stack([compress_keys, compress_values])
     totals = piece_grad + compress[:, :, None, :, :] * comp_own[:, :, :, None, :]
@@ -346,7 +369,15 @@
         comp_own[:, :, :, None, :] * local.reshape(piece_grad.shape).astype(jnp.float32), axis=2
     )
     gate_part = gate_acc.transpose(0, 2, 1, 3).reshape(kv_heads * group, 2, head_dim)
-    summed = lax.psum((weight_grads, gate_part), ("ctx", "dp"))
+    flat = jnp.concatenate(
+        [weight_grads.reshape(-1, head_dim), gate_part.reshape(-1, head_dim)], axis=0
+    )
+    flat = sum_everywhere(flat, ("ctx", "dp"))
+    weight_rows = 2 * kv_heads * span
+    summed = (
+        flat[:weight_rows].reshape(weight_grads.shape),
+        flat[weight_rows:].reshape(gate_part.shape),
+    )
     divisor = math.sqrt(lax.axis_size("dp") * ctx_count * tokens_dev)
     return (
         grads[0][None],

time: 277 us -> 194 us (0.70)
  blocking collectives: 73 us -> 11.2 us
  between operations: 14.3 us -> 0.98 us
  waiting for transfers between devices: 66 us -> 53.6 us
  starting transfers between devices: 14.3 us -> 21.9 us
    psum x1 -> x0, waiting for transfers between devices: 64 us -> none  [on_device(): summed = lax.psum((weight_grads, gate_part), ('ctx', 'dp'))]
    psum x1 -> x0, blocking collectives: 45.3 us -> none  [on_device(): summed = lax.psum((weight_grads, gate_part), ('ctx', 'dp'))]
    all_to_all x1 -> x3, waiting for transfers between devices: 0.01 us -> 28 us  [the longest x1 22.6 us: on_device(): lax.all_to_all(jnp.concatenate([send, comp_send], axis=1), 'ctx', split_a...]
    all_gather x1 -> x0, blocking collectives: 27.7 us -> none  [on_device(): lax.all_gather(comp_local, 'ctx', axis=1, tiled=True).transpose(0, 2, 1, 3)]
    all_to_all x1, waiting for transfers between devices: 0.01 us -> 24.1 us  [on_device(): lax.all_to_all(back, 'ctx', split_axis=0, concat_axis=0, tiled=True)]
    all_to_all x0 -> x1, blocking collectives: none -> 11.2 us  [sum_everywhere(): lax.all_to_all(padded, axes, split_axis=0, concat_axis=0, tiled=True)]
    all_to_all x1 -> x3, starting transfers between devices: 3.66 us -> 10.4 us  [the longest x1 3.74 us: on_device(): lax.all_to_all(jnp.concatenate([send, comp_send], axis=1), 'ctx', split_a...]
    unnamed x19 -> x27, local copies, waits for them, and re-layouts: 8 us -> 6.67 us
  transfers between devices with their start and end apart: 5 -> 5, of which waited for: 2 -> 4; matrix products, arithmetic and copies ran while one was open for 6% -> 10% of each run, Pallas kernels for 0% -> 0%
where the time goes in v2:
time: 194 us; the launch traced here: 193 us
  Pallas kernels  71.4 us (37%)
  waiting for transfers between devices  53.6 us (28%)
  local copies, waits for them, and re-layouts  23.4 us (12%)
  starting transfers between devices  21.9 us (11%)
  blocking collectives  11.2 us (6%)
  other arithmetic  8.51 us (4%)
  matrix products  1.99 us (1%)
    pallas_call x1, Pallas kernels, attend(): pl.pallas_call(functools.partial(attend_kernel, dims), grid=(own_blocks,)...  71.4 us
    all_to_all x1, waiting for transfers between devices, on_device(): lax.all_to_all(back, 'ctx', split_axis=0, concat_axis=0, tiled=True)  24.1 us
    all_to_all x1, waiting for transfers between devices, on_device(): lax.all_to_all(jnp.concatenate([send, comp_send], axis=1), 'ctx', split_a...  22.6 us
    all_to_all x1, blocking collectives, sum_everywhere(): lax.all_to_all(padded, axes, split_axis=0, concat_axis=0, tiled=True)  11.2 us
    unnamed x27, local copies, waits for them, and re-layouts  6.67 us
    all_to_all x1, starting transfers between devices, on_device(): lax.all_to_all(request.transpose(1, 0, 2), 'ctx', split_axis=0, concat_ax...  6.32 us
    all_to_all x1, waiting for transfers between devices, sum_everywhere(): every = lax.all_to_all(mine, axes, split_axis=0, concat_axis=0, tiled=True)  5.4 us
    all_to_all x1, starting transfers between devices, on_device(): lax.all_to_all(back, 'ctx', split_axis=0, concat_axis=0, tiled=True)  5.18 us
  transfers between devices with their start and end apart: 5, of which 4 were waited for; matrix products, arithmetic and copies ran while one was open for 10% of the time, Pallas kernels for 0%

profile of v2, /device:TPU:0, one launch (start us, length us, event | category | flops | bytes accessed | tf_op | source)
XLA Modules:
  0.0 193.0 jit_solution(11874783410670823101)
XLA Ops:
  0.7 0.8 fusion.8
  1.6 0.1 multiply_reduce_fusion.3
  1.7 0.2 select_reduce_fusion
  1.9 0.6 copy.182
  2.5 6.3 %all-to-all-start = ((s32[4,2,4]{2,1,0:T(2,128)}), s32[4,2,4]{2,1,0:T(2,128)S(1)}, u32[]{:S(2)}, u32[]{:S(2)}) async-start(s32[4,2,4]{2,1,0:T(2,128)} %copy.182), calls=%async_computation | async-start | bytes 8192 | tf_op jit(solution)/shard_map/all_to_all | solution.py:288
  8.9 1.0 copy.178
  9.9 1.0 copy.180
  10.8 0.9 multiply_reduce_fusion.2
  11.8 0.3 copy_bitcast_fusion.1
  12.3 0.5 copy-done
  12.8 0.1 copy.183
  12.9 1.5 all-to-all-done
  14.5 0.8 gather_fusion.1
  15.3 1.0 pad_maximum_fusion
  16.4 3.7 %all-to-all-start.1 = ((bf16[4,1056,128]{2,1,0:T(8,128)(2,1)}), bf16[4,1056,128]{2,1,0:T(8,128)(2,1)S(1)}, u32[]{:S(2)}, u32[]{:S(2)}) async-start(bf16[4,1056,128]{2,1,0:T(8,128)(2,1)} %pad_maximum_fusion), calls=%async_computation.1 | async-start | bytes 2162688 | tf_op jit(solution)/shard_map/all_to_all | solution.py:295
  20.2 0.1 convolution_bitcast_fusion
  20.4 0.6 gather_fusion
  21.2 0.7 select_n.68.bias_ref
  21.8 0.6 copy.234
  22.4 0.9 copy.185
  23.4 22.6 %all-to-all-done.1 = bf16[4,1056,128]{2,1,0:T(8,128)(2,1)S(1)} async-done(((bf16[4,1056,128]{2,1,0:T(8,128)(2,1)}), bf16[4,1056,128]{2,1,0:T(8,128)(2,1)S(1)}, u32[]{:S(2)}, u32[]{:S(2)}) %all-to-all-start.1) | async-done | bytes 1081376 | tf_op jit(solution)/shard_map/all_to_all | solution.py:295
  46.1 0.7 gather_fusion.2
  46.9 0.6 copy.235
  47.5 0.6 copy.236
  48.1 1.2 fusion.6
  49.2 71.4 %shard_map.119 = (f32[2,1280,128]{2,1,0:T(8,128)}, f32[2,1280,128]{2,1,0:T(8,128)}, f32[2,32,128]{2,1,0:T(8,128)}, f32[2,32,128]{2,1,0:T(8,128)}, f32[2,2,8,128]{3,2,1,0:T(8,128)}) custom-call(f32[320]{0:T(512)} %select_n.68.bias_ref, bf16[512,16,128]{2,1,0:T(8,128)(2,1)} %bitcast.146, bf16[512,16,128]{2,1,0:T(8,128)(2,1)} %bitcast.147, ...), custom_call_target="tpu_custom_call" | custom-call | flops 13421772800 | bytes 8388608 | tf_op jit(solution)/shard_map/pallas_call | solution.py:210
  120.7 1.4 copy_bitcast_fusion.3
  122.1 3.3 %all-to-all-start.3 = ((f32[4,2,2,8,128]{4,3,2,1,0:T(8,128)}), f32[4,2,2,8,128]{4,3,2,1,0:T(8,128)S(1)}, u32[]{:S(2)}, u32[]{:S(2)}) async-start(f32[4,2,2,8,128]{4,3,2,1,0:T(8,128)} %copy_bitcast_fusion.3), calls=%async_computation.3 | async-start | bytes 131072 | tf_op jit(solution)/shard_map/all_to_all | solution.py:356
  125.4 2.2 %copy_dynamic-update-slice_fusion.1 = f32[2,2,20,64,128]{4,2,3,0,1:T(8,128)S(1)} fusion(f32[1,2,20,64,128]{4,3,2,1,0:T(8,128)} %bitcast.115), kind=kLoop, calls=%fused_computation.6 | loop fusion | bytes 2883584
  127.6 0.8 copy_dynamic-update-slice_fusion
  128.4 0.1 slice.85
  128.5 0.2 copy.192
  128.8 1.2 concatenate.24
  130.0 2.9 %gather_fusion.3 = bf16[4,2,4,2,64,128]{5,4,3,2,1,0:T(8,128)(2,1)} fusion(bf16[4,2,4,2,64,128]{5,4,3,2,1,0:T(8,128)(2,1)} %concatenate.24, s32[1024]{0:T(1024)S(1)} %pad_clamp_fusion), kind=kCustom, calls=%fused_computation.3 | custom fusion | bytes 2097168 | tf_op jit(solution)/shard_map/gather | solution.py:345
  132.8 3.1 %copy.194 = bf16[4,2,4,2,64,128]{5,2,4,3,1,0:T(4,128)(2,1)} copy(bf16[4,2,4,2,64,128]{5,4,3,2,1,0:T(8,128)(2,1)} %gather_fusion.3) | data formatting | bytes 2097152 | tf_op jit(solution)/shard_map/convert_element_type | solution.py:345
  136.0 5.2 %all-to-all-start.2 = ((bf16[4,2,4,2,64,128]{5,2,4,3,1,0:T(4,128)(2,1)}), bf16[4,2,4,2,64,128]{5,2,4,3,1,0:T(4,128)(2,1)}, u32[]{:S(2)}, u32[]{:S(2)}) async-start(bf16[4,2,4,2,64,128]{5,2,4,3,1,0:T(4,128)(2,1)} %copy.194), calls=%async_computation.2 | async-start | bytes 2097152 | tf_op jit(solution)/shard_map/all_to_all | solution.py:346
  141.2 0.6 copy.203
  141.8 24.1 %all-to-all-done.2 = bf16[4,2,4,2,64,128]{5,2,4,3,1,0:T(4,128)(2,1)} async-done(((bf16[4,2,4,2,64,128]{5,2,4,3,1,0:T(4,128)(2,1)}), bf16[4,2,4,2,64,128]{5,2,4,3,1,0:T(4,128)(2,1)}, u32[]{:S(2)}, u32[]{:S(2)}) %all-to-all-start.2) | async-done | bytes 1048608 | tf_op jit(solution)/shard_map/all_to_all | solution.py:346
  165.9 1.9 fusion.2
  167.8 1.2 multiply_reduce_fusion
  169.0 11.2 %all_to_all.30 = f32[8,40,128]{2,1,0:T(8,128)S(1)} all-to-all(f32[8,40,128]{2,1,0:T(8,128)S(1)} %bitcast.118), channel_id=1, replica_groups=mesh['groups'=2,'ctx'=4,'dp'=2,'head'=2] {'ctx','dp'}, dimensions={0} | all-to-all | bytes 327680 | tf_op jit(solution)/shard_map/all_to_all | solution.py:239
  180.2 0.7 broadcast_in_dim.22
  180.9 3.4 %all-to-all-start.5 = ((f32[8,40,128]{2,1,0:T(8,128)}), f32[8,40,128]{2,1,0:T(8,128)S(1)}, u32[]{:S(2)}, u32[]{:S(2)}) async-start(f32[8,40,128]{2,1,0:T(8,128)} %broadcast_in_dim.22), calls=%async_computation.5 | async-start | bytes 327680 | tf_op jit(solution)/shard_map/all_to_all | solution.py:241
  184.4 1.0 copy.205
  185.4 1.0 copy.204
  186.4 5.4 %all-to-all-done.5 = f32[8,40,128]{2,1,0:T(8,128)S(1)} async-done(((f32[8,40,128]{2,1,0:T(8,128)}), f32[8,40,128]{2,1,0:T(8,128)S(1)}, u32[]{:S(2)}, u32[]{:S(2)}) %all-to-all-start.5) | async-done | bytes 163872 | tf_op jit(solution)/shard_map/all_to_all | solution.py:241
  191.8 0.6 slice_multiply_fusion.2
  192.4 0.7 slice_multiply_fusion
  (57 shorter events, 1.1 us)
Async XLA Ops:
  0.6 11.5 %copy-start.5 = (f32[2,64,128]{2,1,0:T(8,128)S(1)}, f32[2,64,128]{2,1,0:T(8,128)}, u32[]{:S(2)}) copy-start(f32[2,64,128]{2,1,0:T(8,128)} %param.14) | copy-start | bytes 196612
  2.5 11.9 %all-to-all-start = ((s32[4,2,4]{2,1,0:T(2,128)}), s32[4,2,4]{2,1,0:T(2,128)S(1)}, u32[]{:S(2)}, u32[]{:S(2)}) async-start(s32[4,2,4]{2,1,0:T(2,128)} %copy.182), calls=%async_computation | async-start | bytes 8192 | tf_op jit(solution)/shard_map/all_to_all | solution.py:288
  12.1 0.7 copy-start
  14.4 0.9 copy-start.10
  16.4 5.5 %copy-start.8 = (f32[16,2,128]{2,1,0:T(2,128)S(1)}, f32[16,2,128]{2,1,0:T(2,128)}, u32[]{:S(2)}) copy-start(f32[16,2,128]{2,1,0:T(2,128)} %param.15) | copy-start | bytes 49156
  16.4 29.6 %all-to-all-start.1 = ((bf16[4,1056,128]{2,1,0:T(8,128)(2,1)}), bf16[4,1056,128]{2,1,0:T(8,128)(2,1)S(1)}, u32[]{:S(2)}, u32[]{:S(2)}) async-start(bf16[4,1056,128]{2,1,0:T(8,128)(2,1)} %pad_maximum_fusion), calls=%async_computation.1 | async-start | bytes 2162688 | tf_op jit(solution)/shard_map/all_to_all | solution.py:295
  46.8 1.3 copy-start.2
  122.1 13.9 %all-to-all-start.3 = ((f32[4,2,2,8,128]{4,3,2,1,0:T(8,128)}), f32[4,2,2,8,128]{4,3,2,1,0:T(8,128)S(1)}, u32[]{:S(2)}, u32[]{:S(2)}) async-start(f32[4,2,2,8,128]{4,3,2,1,0:T(8,128)} %copy_bitcast_fusion.3), calls=%async_computation.3 | async-start | bytes 131072 | tf_op jit(solution)/shard_map/all_to_all | solution.py:356
  125.4 2.2 %copy-start.4 = (f32[2,1280,128]{2,1,0:T(8,128)S(1)}, f32[2,1280,128]{2,1,0:T(8,128)}, u32[]{:S(2)}) copy-start(f32[2,1280,128]{2,1,0:T(8,128)} %get-tuple-element.11) | copy-start | bytes 3932164
  136.0 5.2 %copy-start.9 = (f32[2,2,8,128]{3,2,1,0:T(8,128)S(1)}, f32[2,2,8,128]{3,2,1,0:T(8,128)}, u32[]{:S(2)}) copy-start(f32[2,2,8,128]{3,2,1,0:T(8,128)} %get-tuple-element.14) | copy-start | bytes 49156
  136.0 29.9 %all-to-all-start.2 = ((bf16[4,2,4,2,64,128]{5,2,4,3,1,0:T(4,128)(2,1)}), bf16[4,2,4,2,64,128]{5,2,4,3,1,0:T(4,128)(2,1)}, u32[]{:S(2)}, u32[]{:S(2)}) async-start(bf16[4,2,4,2,64,128]{5,2,4,3,1,0:T(4,128)(2,1)} %copy.194), calls=%async_computation.2 | async-start | bytes 2097152 | tf_op jit(solution)/shard_map/all_to_all | solution.py:346
  141.8 26.0 %copy-start.6 = (f32[2,64,128]{2,1,0:T(8,128)S(1)}, f32[2,64,128]{2,1,0:T(8,128)}, u32[]{:S(2)}) copy-start(f32[2,64,128]{2,1,0:T(8,128)} %param.13) | copy-start | bytes 196612
  165.9 1.9 copy-start.1
  167.8 1.2 copy-start.7
  169.0 15.3 %copy-start.3 = (bf16[2,8,64,2,128]{4,1,2,0,3:T(8,128)(2,1)S(1)}, bf16[2,8,64,2,128]{4,1,2,0,3:T(8,128)(2,1)}, u32[]{:S(2)}) copy-start(bf16[2,8,64,2,128]{4,1,2,0,3:T(8,128)(2,1)} %get-tuple-element.56) | copy-start | bytes 1572868
  180.9 10.9 %all-to-all-start.5 = ((f32[8,40,128]{2,1,0:T(8,128)}), f32[8,40,128]{2,1,0:T(8,128)S(1)}, u32[]{:S(2)}, u32[]{:S(2)}) async-start(f32[8,40,128]{2,1,0:T(8,128)} %broadcast_in_dim.22), calls=%async_computation.5 | async-start | bytes 327680 | tf_op jit(solution)/shard_map/all_to_all | solution.py:241

commit v3 on v2

--- a/solution.py
+++ b/solution.py
@@ -17,6 +17,21 @@
 
 def dot(a, b, dims):
     return lax.dot_general(a, b, dims, preferred_element_type=jnp.float32)
+
+
+UNROLL = 20
+
+
+def span_of(c, size):
+    return pl.ds(c * size if isinstance(c, int) else pl.multiple_of(c * size, size), size)
+
+
+def sweep(slots, chunk_slots, used, body, start):
+    if slots <= UNROLL:
+        for c in range(slots // chunk_slots):
+            start = body(c, start)
+        return start
+    return lax.fori_loop(0, used, body, start)
 
 
 def fold(x, op):
@@ -45,7 +60,7 @@
     ot_scr,
     tri_scr,
 ):
-    kv_heads, group, span, remote_slots, own_blocks, chunk_slots, pair = dims
+    kv_heads, group, span, remote_slots, own_blocks, chunk_slots, pair, offset = dims
     slots = remote_slots + own_blocks
     chunk = chunk_slots * span
     head_dim = q_ref.shape[-1]
@@ -67,7 +82,7 @@
         tri_scr[...] = jnp.where(key_at <= row_at, 0.0, MASKED)
 
         def turn(c, _):
-            at = pl.ds(pl.multiple_of(c * chunk, chunk), chunk)
+            at = span_of(c, chunk)
             for g in range(kv_heads):
                 vt_scr[g, :, at] = v_ref[g, at, :].astype(jnp.float32).T.astype(jnp.bfloat16)
             return 0
@@ -80,12 +95,12 @@
         narrow = {}
         for p, g in heads:
             wide[p] = (
-                q_ref[...].astype(jnp.float32)[:, g * group : (g + 1) * group, :]
+                q_ref[...].astype(jnp.float32)[:, (offset + g) * group : (offset + g + 1) * group, :]
             )
             narrow[p] = wide[p].reshape(rows, head_dim).astype(jnp.bfloat16)
 
         def scores(c, peaks):
-            at = pl.ds(pl.multiple_of(c * chunk, chunk), chunk)
+            at = span_of(c, chunk)
             out = []
             for p, g in heads:
                 s = dot(k_ref[g, at, :], narrow[p], NT)
@@ -98,8 +113,8 @@
                 out.append(jnp.maximum(peaks[p], fold(s, jnp.max)))
             return tuple(out)
 
-        peaks = lax.fori_loop(
-            0, chunks, scores, tuple(jnp.full((8, rows), MASKED, jnp.float32) for _ in heads)
+        peaks = sweep(
+            slots, chunk_slots, chunks, scores, tuple(jnp.full((8, rows), MASKED, jnp.float32) for _ in heads)
         )
         own = pl.ds(pl.multiple_of((remote_slots + j) * span, span), span)
         peak = {}
@@ -111,7 +126,7 @@
             )
 
         def raise_all(c, sums):
-            at = pl.ds(pl.multiple_of(c * chunk, chunk), chunk)
+            at = span_of(c, chunk)
             out = []
             for p, g in heads:
                 e = jnp.exp2((s_scr[p, at, :] - peak[p]) * power)
@@ -119,21 +134,21 @@
                 out.append(sums[p] + fold(e, jnp.sum))
             return tuple(out)
 
-        sums = lax.fori_loop(
-            0, chunks, raise_all, tuple(jnp.zeros((8, rows), jnp.float32) for _ in heads)
+        sums = sweep(
+            slots, chunk_slots, chunks, raise_all, tuple(jnp.zeros((8, rows), jnp.float32) for _ in heads)
         )
         inverse = {p: 1.0 / jnp.sum(sums[p], axis=0, keepdims=True) for p, g in heads}
         ot_scr[...] = jnp.zeros_like(ot_scr)
 
         def outputs(c, _):
-            at = pl.ds(pl.multiple_of(c * chunk, chunk), chunk)
+            at = span_of(c, chunk)
             for p, g in heads:
                 w = s_scr[p, at, :] * inverse[p]
                 s_scr[p, at, :] = w
                 ot_scr[p] += dot(vt_scr[g, :, at], w.astype(jnp.bfloat16), NN)
             return 0
 
-        lax.fori_loop(0, chunks, outputs, 0)
+        sweep(slots, chunk_slots, chunks, outputs, 0)
 
         backs = {}
         for p, g in heads:
@@ -141,8 +156,9 @@
             ck = ck_ref[g]
             cv = cv_ref[g]
             cs = dot(ck, narrow[p], NT)
+            all_blocks = cs.shape[0]
             at_block = lax.broadcasted_iota(jnp.int32, cs.shape, 0)
-            usable = at_block <= cur_ref[0] + j
+            usable = (at_block + cur_ref[0] >= 0) & (at_block <= all_blocks - own_blocks + j)
             cs = jnp.where(usable, cs, MASKED)
             ce = jnp.exp2((cs - jnp.max(cs, axis=0, keepdims=True)) * power)
             cw = ce * (1.0 / jnp.sum(ce, axis=0, keepdims=True))
@@ -155,7 +171,9 @@
                 gates.append(jax.nn.sigmoid(logit))
             comp3 = comp_out.reshape(span, group, head_dim)
             sel3 = sel_out.reshape(span, group, head_dim)
-            t3 = t_ref[...].astype(jnp.float32)[:, g * group : (g + 1) * group, :]
+            t3 = t_ref[...].astype(jnp.float32)[
+                :, (offset + g) * group : (offset + g + 1) * group, :
+            ]
             error = gates[0] * comp3 + gates[1] * sel3 - t3
             for r, branch in ((0, comp3), (1, sel3)):
                 term = jnp.sum(error * branch, axis=-1, keepdims=True) * (
@@ -171,7 +189,7 @@
             dcv_ref[g] += dot(cr, cb, NN)
 
         def weight_grads(c, totals):
-            at = pl.ds(pl.multiple_of(c * chunk, chunk), chunk)
+            at = span_of(c, chunk)
             out = []
             for p, g in heads:
                 d = dot(v_ref[g, at, :], backs[p], NT)
@@ -179,13 +197,13 @@
                 out.append(totals[p] + fold(s_scr[p, at, :] * d, jnp.sum))
             return tuple(out)
 
-        totals = lax.fori_loop(
-            0, chunks, weight_grads, tuple(jnp.zeros((8, rows), jnp.float32) for _ in heads)
+        totals = sweep(
+            slots, chunk_slots, chunks, weight_grads, tuple(jnp.zeros((8, rows), jnp.float32) for _ in heads)
         )
         total = {p: jnp.sum(totals[p], axis=0, keepdims=True) for p, g in heads}
 
         def key_grads(c, _):
-            at = pl.ds(pl.multiple_of(c * chunk, chunk), chunk)
+            at = span_of(c, chunk)
             for p, g in heads:
                 w = s_scr[p, at, :]
                 sg = (w * ((d_scr[p, at, :] - total[p]) * factor)).astype(jnp.bfloat16)
@@ -193,18 +211,18 @@
                 dv_ref[g, at, :] += dot(w.astype(jnp.bfloat16), backs[p], NN)
             return 0
 
-        lax.fori_loop(0, chunks, key_grads, 0)
+        sweep(slots, chunk_slots, chunks, key_grads, 0)
 
 
 def attend(queries, teacher, keys, values, comp_keys, comp_values, gate_pairs, bias, first, dims):
-    kv_heads, group, span, remote_slots, own_blocks, chunk_slots, pair = dims
+    kv_heads, group, span, remote_slots, own_blocks, chunk_slots, pair, offset = dims
     slots = remote_slots + own_blocks
     head_dim = keys.shape[-1]
     all_blocks = comp_keys.shape[1]
     rows = span * group
     whole = pl.BlockSpec(memory_space=pltpu.VMEM)
     scalars = pl.BlockSpec(memory_space=pltpu.SMEM)
-    tokens = pl.BlockSpec((span, kv_heads * group, head_dim), lambda j: (j, 0, 0))
+    tokens = pl.BlockSpec((span, queries.shape[1], head_dim), lambda j: (j, 0, 0))
     f32 = jnp.float32
     flops = own_blocks * kv_heads * rows * slots * span * head_dim * 10
     return pl.pallas_call(
@@ -261,20 +279,15 @@
     own_blocks = tokens_dev // span
     all_blocks = own_blocks * ctx_count
     group = queries.shape[2] // kv_heads
-    key_blocks = key_states[0].reshape(own_blocks, span, kv_heads, head_dim)
-    value_blocks = value_states[0].reshape(own_blocks, span, kv_heads, head_dim)
-    comp_local = jnp.stack(
-        [
-            jnp.sum(key_blocks.astype(jnp.float32) * compress_keys.transpose(1, 0, 2)[None], axis=1),
-            jnp.sum(
-                value_blocks.astype(jnp.float32) * compress_values.transpose(1, 0, 2)[None], axis=1
-            ),
-        ]
+    both = jnp.stack([key_states[0], value_states[0]]).reshape(
+        2, own_blocks, span, kv_heads, head_dim
+    )
+    compress = jnp.stack([compress_keys, compress_values])
+    comp_local = jnp.sum(
+        both.astype(jnp.float32) * compress.transpose(0, 2, 1, 3)[:, None], axis=2
     ).astype(jnp.bfloat16)
+    local = both.transpose(3, 0, 1, 2, 4)
     chosen = selection[0]
-    pieces = jnp.stack(
-        [key_blocks.transpose(2, 0, 1, 3), value_blocks.transpose(2, 0, 1, 3)], axis=2
-    )
     capacity = own_blocks // 2
     hits = jnp.any(chosen[..., None] == jnp.arange(all_blocks), axis=2)
     hits = hits.astype(jnp.int32).reshape(own_blocks, kv_heads, ctx_count, own_blocks)
@@ -288,24 +301,11 @@
     asked = lax.all_to_all(
         request.transpose(1, 0, 2), "ctx", split_axis=0, concat_axis=0, tiled=True
     )
-    head_pick = jnp.arange(kv_heads)[None, :, None]
-    send = pieces[head_pick, asked].reshape(ctx_count, -1, head_dim)
-    comp_rows = comp_local.transpose(0, 2, 1, 3).reshape(-1, head_dim)
-    comp_send = jnp.broadcast_to(comp_rows[None], (ctx_count,) + comp_rows.shape)
-    mixed = lax.all_to_all(
-        jnp.concatenate([send, comp_send], axis=1), "ctx", split_axis=0, concat_axis=0, tiled=True
-    )
-    got = mixed[:, : send.shape[1]].reshape(ctx_count, kv_heads, capacity, 2, span, head_dim)
-    comp_all = mixed[:, send.shape[1] :].reshape(ctx_count, 2, kv_heads, own_blocks, head_dim)
-    comp_all = comp_all.transpose(1, 2, 0, 3, 4).reshape(2, kv_heads, all_blocks, head_dim)
-    comp_keys, comp_values = comp_all[0], comp_all[1]
-    others = (my_index + 1 + jnp.arange(ctx_count - 1)) % ctx_count
-    got = got[others]
+    shifts = range(1, ctx_count)
+    above = asked[(my_index + jnp.arange(1, ctx_count)) % ctx_count]
+    others = (my_index - jnp.arange(1, ctx_count)) % ctx_count
     remote_slots = (ctx_count - 1) * capacity
     slots = remote_slots + own_blocks
-    got = got.transpose(3, 1, 0, 2, 4, 5).reshape(2, kv_heads, remote_slots * span, head_dim)
-    local = pieces.transpose(2, 0, 1, 3, 4).reshape(2, kv_heads, tokens_dev, head_dim)
-    both = jnp.concatenate([got, local], axis=2)
     slot_on = jnp.einsum("jhob,hobc->jhoc", hits, slot_hit)[:, :, others].reshape(
         own_blocks, kv_heads, remote_slots
     )
@@ -313,62 +313,80 @@
     below = jnp.arange(own_blocks)[None, :] < jnp.arange(own_blocks)[:, None]
     local_on = local_on * below.astype(jnp.int32)[:, None, :]
     bias = jnp.where(jnp.concatenate([slot_on, local_on], axis=-1) > 0, 0.0, MASKED)
-    bias = bias.astype(jnp.float32).reshape(-1)
-    dims = (
-        kv_heads,
-        group,
-        span,
-        remote_slots,
-        own_blocks,
-        capacity,
-        kv_heads if slots <= 40 else 1,
-    )
+    bias = bias.astype(jnp.float32)
     gate_pairs = gate_weights.reshape(kv_heads, group, 2, head_dim).transpose(0, 2, 1, 3)
-    first = (my_index * own_blocks).astype(jnp.int32).reshape(1)
-    key_acc, value_acc, comp_key_acc, comp_value_acc, gate_acc = attend(
-        queries[0],
-        teacher_out[0],
-        both[0],
-        both[1],
-        comp_keys,
-        comp_values,
-        gate_pairs,
-        bias,
-        first,
-        dims,
-    )
-    accs = jnp.stack([key_acc, value_acc]).reshape(2, kv_heads, slots, span, head_dim)
-    back = accs[:, :, :remote_slots].reshape(
-        2, kv_heads, ctx_count - 1, capacity, span, head_dim
-    ).transpose(2, 1, 3, 0, 4, 5)
-    back = jnp.concatenate([back, jnp.zeros_like(back[:1])], axis=0)
-    back = back[(jnp.arange(ctx_count) - my_index - 1) % ctx_count].astype(jnp.bfloat16)
-    returned = lax.all_to_all(back, "ctx", split_axis=0, concat_axis=0, tiled=True)
-    place = (asked[..., None] == jnp.arange(own_blocks)).astype(jnp.bfloat16)
-    added = jnp.einsum(
-        "ohcb,ohcrud->rhbud", place, returned, preferred_element_type=jnp.float32
-    )
-    piece_grad = accs[:, :, remote_slots:] + added
-    comp_parts = jnp.stack([comp_key_acc, comp_value_acc]).reshape(
-        2, kv_heads, ctx_count, own_blocks, head_dim
-    )
-    comp_own = jnp.sum(
-        lax.all_to_all(
-            comp_parts.transpose(2, 0, 1, 3, 4), "ctx", split_axis=0, concat_axis=0, tiled=True
-        ),
-        axis=0,
-    )
-    compress = jnp.stack([compress_keys, compress_values])
-    totals = piece_grad + compress[:, :, None, :, :] * comp_own[:, :, :, None, :]
-    grads = (
-        totals.transpose(0, 2, 3, 1, 4)
-        .reshape(2, tokens_dev, kv_heads, head_dim)
-        .astype(jnp.bfloat16)
-    )
-    weight_grads = jnp.sum(
-        comp_own[:, :, :, None, :] * local.reshape(piece_grad.shape).astype(jnp.float32), axis=2
-    )
-    gate_part = gate_acc.transpose(0, 2, 1, 3).reshape(kv_heads * group, 2, head_dim)
+    first = ((my_index - ctx_count + 1) * own_blocks).astype(jnp.int32).reshape(1)
+    piece_rows = capacity * span
+
+    def up(x, shift):
+        return lax.ppermute(x, "ctx", [(i, i + shift) for i in range(ctx_count - shift)])
+
+    def down(x, shift):
+        return lax.ppermute(x, "ctx", [(i + shift, i) for i in range(ctx_count - shift)])
+
+    arrived = []
+    for h in range(kv_heads):
+        parts = []
+        for shift in shifts:
+            picked = local[h][:, above[shift - 1, h]].reshape(2, piece_rows, head_dim)
+            parts.append(up(jnp.concatenate([picked, comp_local[:, :, h]], axis=1), shift))
+        arrived.append(parts)
+    key_value_back = []
+    comp_sums = []
+    gate_sums = []
+    for h in range(kv_heads):
+        parts = arrived[h]
+        pieces = jnp.concatenate(
+            [part[:, :piece_rows] for part in parts] + [local[h].reshape(2, -1, head_dim)], axis=1
+        )
+        comp = jnp.concatenate(
+            [part[:, piece_rows:] for part in parts[::-1]] + [comp_local[:, :, h]], axis=1
+        )
+        dims = (
+            1,
+            group,
+            span,
+            remote_slots,
+            own_blocks,
+            slots if slots <= UNROLL else capacity,
+            1,
+            h,
+        )
+        key_acc, value_acc, comp_key, comp_value, gate_acc = attend(
+            queries[0],
+            teacher_out[0],
+            pieces[0][None],
+            pieces[1][None],
+            comp[0][None],
+            comp[1][None],
+            gate_pairs[h][None],
+            bias[:, h].reshape(-1),
+            first,
+            dims,
+        )
+        if key_value_back:
+            own, returned = key_value_back[-1]
+            key_acc, value_acc, comp_key, comp_value, gate_acc, returned = lax.optimization_barrier(
+                (key_acc, value_acc, comp_key, comp_value, gate_acc, returned)
+            )
+            key_value_back[-1] = (own, returned)
+        accs = jnp.concatenate([key_acc, value_acc])
+        returned = [
+            down(
+                accs[:, (shift - 1) * piece_rows : shift * piece_rows].astype(jnp.bfloat16), shift
+            )
+            for shift in shifts
+        ]
+        key_value_back.append((accs[:, remote_slots * span :], returned))
+        comp_sums.append(jnp.concatenate([comp_key, comp_value]))
+        gate_sums.append(gate_acc[0])
+    comp_acc = jnp.stack(comp_sums).reshape(kv_heads, 2, ctx_count, own_blocks, head_dim)
+    comp_own = comp_acc[:, :, ctx_count - 1]
+    for shift in shifts:
+        comp_own = comp_own + down(comp_acc[:, :, ctx_count - 1 - shift], shift)
+    weight_grads = jnp.sum(comp_own[:, :, :, None, :] * local.astype(jnp.float32), axis=2)
+    weight_grads = weight_grads.transpose(1, 0, 2, 3)
+    gate_part = jnp.stack(gate_sums).transpose(0, 2, 1, 3).reshape(kv_heads * group, 2, head_dim)
     flat = jnp.concatenate(
         [weight_grads.reshape(-1, head_dim), gate_part.reshape(-1, head_dim)], axis=0
     )
@@ -378,6 +396,17 @@
         flat[:weight_rows].reshape(weight_grads.shape),
         flat[weight_rows:].reshape(gate_part.shape),
     )
+    totals = []
+    for h in range(kv_heads):
+        own, returned = key_value_back[h]
+        place = (above[:, h, :, None] == jnp.arange(own_blocks)).astype(jnp.bfloat16)
+        place = place.transpose(2, 0, 1).reshape(own_blocks, remote_slots)
+        stacked = jnp.stack(returned, axis=1).reshape(2, remote_slots, span, head_dim)
+        added = jnp.einsum("bs,tsud->tbud", place, stacked, preferred_element_type=jnp.float32)
+        total = own.reshape(added.shape) + added
+        totals.append(total + compress[:, h][:, None] * comp_own[h][:, :, None, :])
+    grads = jnp.stack(totals, axis=3).astype(jnp.bfloat16)
+    grads = grads.reshape(2, tokens_dev, kv_heads, head_dim)
     divisor = math.sqrt(lax.axis_size("dp") * ctx_count * tokens_dev)
     return (
         grads[0][None],

time: 194 us -> 155 us (0.80)
  waiting for transfers between devices: 53.6 us -> 21.1 us
  starting transfers between devices: 21.9 us -> 41.5 us
  blocking collectives: 11.2 us -> 0 us
  local copies, waits for them, and re-layouts: 23.4 us -> 16 us
  Pallas kernels: 71.4 us -> 66.3 us
    all_to_all x3 -> x1, waiting for transfers between devices: 46.7 us -> 1.19 us  [sum_everywhere(): lax.all_to_all(padded, axes, split_axis=0, concat_axis=0, tiled=True)]
    ppermute x0 -> x15, starting transfers between devices: none -> 25 us  [the longest x6 13.2 us: up(): lax.ppermute(x, 'ctx', [(i, i + shift) for i in range(ctx_count - shift)])]
    ppermute x0 -> x15, waiting for transfers between devices: none -> 14.9 us  [the longest x9 14.8 us: down(): lax.ppermute(x, 'ctx', [(i + shift, i) for i in range(ctx_count - shift)])]
    all_to_all x1 -> x0, blocking collectives: 11.2 us -> none  [sum_everywhere(): lax.all_to_all(padded, axes, split_axis=0, concat_axis=0, tiled=True)]
    all_to_all x3 -> x1, starting transfers between devices: 12.2 us -> 6.76 us  [sum_everywhere(): lax.all_to_all(padded, axes, split_axis=0, concat_axis=0, tiled=True)]
    pallas_call x1 -> x2, Pallas kernels: 71.4 us -> 66.3 us  [attend(): pl.pallas_call(functools.partial(attend_kernel, dims), grid=(own_blocks,)...]
    convert_element_type x1 -> x0, local copies, waits for them, and re-layouts: 3.13 us -> none  [on_device(): back[(jnp.arange(ctx_count) - my_index - 1) % ctx_count]]
    another operation x1 -> x8, other arithmetic: 0.01 us -> 2.95 us  [the longest x1 1.81 us: on_device(): jnp.stack([key_states[0], value_states[0]])]
  transfers between devices with their start and end apart: 5 -> 18, of which waited for: 4 -> 7; matrix products, arithmetic and copies ran while one was open for 10% -> 11% of each run, Pallas kernels for 0% -> 43%
where the time goes in v3:
time: 155 us; the launch traced here: 154 us
  Pallas kernels  66.3 us (43%)
  starting transfers between devices  41.5 us (27%)
  waiting for transfers between devices  21.1 us (14%)
  local copies, waits for them, and re-layouts  16 us (10%)
  other arithmetic  6.72 us (4%)
    pallas_call x2, Pallas kernels, attend(): pl.pallas_call(functools.partial(attend_kernel, dims), grid=(own_blocks,)...  66.3 us
    ppermute x9, waiting for transfers between devices, down(): lax.ppermute(x, 'ctx', [(i + shift, i) for i in range(ctx_count - shift)])  14.8 us
    ppermute x6, starting transfers between devices, up(): lax.ppermute(x, 'ctx', [(i, i + shift) for i in range(ctx_count - shift)])  13.2 us
    ppermute x9, starting transfers between devices, down(): lax.ppermute(x, 'ctx', [(i + shift, i) for i in range(ctx_count - shift)])  11.8 us
    all_to_all x1, starting transfers between devices, sum_everywhere(): lax.all_to_all(padded, axes, split_axis=0, concat_axis=0, tiled=True)  6.76 us
    all_to_all x1, starting transfers between devices, on_device(): lax.all_to_all(request.transpose(1, 0, 2), 'ctx', split_axis=0, concat_ax...  6.32 us
    all_to_all x1, waiting for transfers between devices, sum_everywhere(): every = lax.all_to_all(mine, axes, split_axis=0, concat_axis=0, tiled=True)  4.84 us
    unnamed x24, local copies, waits for them, and re-layouts  3.81 us
  transfers between devices with their start and end apart: 18, of which 7 were waited for; matrix products, arithmetic and copies ran while one was open for 11% of the time, Pallas kernels for 43%

profile of v3, /device:TPU:0, one launch (start us, length us, event | category | flops | bytes accessed | tf_op | source)
XLA Modules:
  0.0 154.2 jit_solution(3387126566777893112)
XLA Ops:
  0.7 0.9 fusion.8
  1.9 0.6 copy.165
  2.6 6.3 %all-to-all-start = ((s32[4,2,4]{2,1,0:T(2,128)}), s32[4,2,4]{2,1,0:T(2,128)S(1)}, u32[]{:S(2)}, u32[]{:S(2)}) async-start(s32[4,2,4]{2,1,0:T(2,128)} %bitcast.177), calls=%async_computation | async-start | bytes 8192 | tf_op jit(solution)/shard_map/all_to_all | solution.py:301
  8.9 1.8 %pad_maximum_fusion.2 = bf16[2,512,2,128]{3,2,1,0:T(2,128)(2,1)S(1)} fusion(bf16[1,512,2,128]{3,2,1,0:T(2,128)(2,1)} %param.10, bf16[1,512,2,128]{3,2,1,0:T(2,128)(2,1)} %param.9), kind=kLoop, calls=%fused_computation.17 | loop fusion | flops 262144 | bytes 1048576 | tf_op jit(solution)/shard_map/stack | solution.py:282
  12.4 0.6 reshape_squeeze.12.bias_ref
  13.0 0.6 fusion.59
  13.6 0.7 reshape_squeeze.14.bias_ref
  15.0 0.6 gather_fusion.2
  15.6 0.6 gather_fusion.3
  16.3 0.6 gather_fusion.4
  16.9 5.6 %collective-permute-start.2 = (bf16[2,264,128]{2,1,0:T(8,128)(2,1)S(1)}, bf16[2,264,128]{2,1,0:T(8,128)(2,1)S(1)}, u32[]{:S(2)}, u32[]{:S(2)}) collective-permute-start(bf16[2,264,128]{2,1,0:T(8,128)(2,1)S(1)} %get-tuple-element.100), channel_id=1, source_target_pairs={{0,12},{1,13},{2,14},{3,15},{16,28},{17,29},{18,30},{19,31}} | collective-permute-start | bytes 405512 | tf_op jit(solution)/shard_map/ppermute | solution.py:322
  22.5 1.3 collective-permute-start.1
  23.8 2.5 %collective-permute-start = (bf16[2,264,128]{2,1,0:T(8,128)(2,1)S(1)}, bf16[2,264,128]{2,1,0:T(8,128)(2,1)S(1)}, u32[]{:S(2)}, u32[]{:S(2)}) collective-permute-start(bf16[2,264,128]{2,1,0:T(8,128)(2,1)S(1)} %get-tuple-element.98), channel_id=1, source_target_pairs={{0,4},{4,8},{8,12},{1,5},{5,9},{9,13},{2,6},{6,10},{10,14},{3,7},{... | collective-permute-start | bytes 405512 | tf_op jit(solution)/shard_map/ppermute | solution.py:322
  26.3 0.6 gather_fusion.5
  26.9 0.6 gather_fusion.6
  28.1 1.3 collective-permute-start.5
  29.4 1.3 collective-permute-start.4
  30.9 1.3 collective-permute-start.3
  32.4 0.6 fusion.60
  33.1 0.9 fusion.57
  34.0 33.1 %shard_map.119 = (f32[1,1280,128]{2,1,0:T(8,128)}, f32[1,1280,128]{2,1,0:T(8,128)}, f32[1,32,128]{2,1,0:T(8,128)}, f32[1,32,128]{2,1,0:T(8,128)}, f32[1,2,8,128]{3,2,1,0:T(8,128)}) custom-call(f32[160]{0:T(256)} %reshape_squeeze.12.bias_ref, bf16[512,16,128]{2,1,0:T(8,128)(2,1)} %bitcast.224, bf16[512,16,128]{2,1,0:T(8,128)(2,1)} %bitcast.226, ...), custom_call_target="tpu_custom_call" | custom-call | flops 6710886400 | bytes 8388608 | tf_op jit(solution)/shard_map/pallas_call | solution.py:228
  67.1 1.2 constant_dynamic-update-slice_fusion.1
  68.6 1.3 collective-permute-start.6
  69.9 1.3 collective-permute-start.7
  71.2 1.3 collective-permute-start.8
  72.5 0.6 fusion.61
  73.2 0.9 fusion.58
  74.2 33.1 %shard_map.120 = (f32[1,1280,128]{2,1,0:T(8,128)}, f32[1,1280,128]{2,1,0:T(8,128)}, f32[1,32,128]{2,1,0:T(8,128)}, f32[1,32,128]{2,1,0:T(8,128)}, f32[1,2,8,128]{3,2,1,0:T(8,128)}) custom-call(f32[160]{0:T(256)} %reshape_squeeze.14.bias_ref, bf16[512,16,128]{2,1,0:T(8,128)(2,1)} %bitcast.225, bf16[512,16,128]{2,1,0:T(8,128)(2,1)} %bitcast.227, ...), custom_call_target="tpu_custom_call" | custom-call | flops 6710886400 | bytes 8388608 | tf_op jit(solution)/shard_map/pallas_call | solution.py:228
  107.4 0.8 maximum_bitcast_fusion.1
  108.3 1.3 collective-permute-start.10
  109.5 1.3 collective-permute-start.11
  110.8 1.5 collective-permute-start.9
  113.3 1.3 collective-permute-start.12
  114.6 1.3 collective-permute-start.13
  115.9 5.8 %collective-permute-done.10 = f32[2,2,8,128]{3,2,1,0:T(8,128)S(1)} collective-permute-done((f32[2,2,8,128]{3,2,1,0:T(8,128)S(1)}, f32[2,2,8,128]{3,2,1,0:T(8,128)S(1)}, u32[]{:S(2)}, u32[]{:S(2)}) %collective-permute-start.10) | collective-permute-done | bytes 16416 | tf_op jit(solution)/shard_map/ppermute | solution.py:325
  121.7 1.3 collective-permute-start.14
  123.0 2.1 %collective-permute-done.11 = f32[2,2,8,128]{3,2,1,0:T(8,128)S(1)} collective-permute-done((f32[2,2,8,128]{3,2,1,0:T(8,128)S(1)}, f32[2,2,8,128]{3,2,1,0:T(8,128)S(1)}, u32[]{:S(2)}, u32[]{:S(2)}) %collective-permute-start.11) | collective-permute-done | bytes 16416 | tf_op jit(solution)/shard_map/ppermute | solution.py:325
  125.3 0.7 select_maximum_fusion
  125.9 6.8 %all-to-all-start.1 = ((f32[8,40,128]{2,1,0:T(8,128)}), f32[8,40,128]{2,1,0:T(8,128)S(1)}, u32[]{:S(2)}, u32[]{:S(2)}) async-start(f32[8,40,128]{2,1,0:T(8,128)} %bitcast.83), calls=%async_computation.1 | async-start | bytes 327680 | tf_op jit(solution)/shard_map/all_to_all | solution.py:257
  133.3 6.8 %collective-permute-done.13 = bf16[2,256,128]{2,1,0:T(8,128)(2,1)S(1)} collective-permute-done((bf16[2,256,128]{2,1,0:T(8,128)(2,1)S(1)}, bf16[2,256,128]{2,1,0:T(8,128)(2,1)S(1)}, u32[]{:S(2)}, u32[]{:S(2)}) %collective-permute-start.13) | collective-permute-done | bytes 131104 | tf_op jit(solution)/shard_map/ppermute | solution.py:325
  140.2 1.2 all-to-all-done.1
  141.4 0.7 broadcast_in_dim.10
  142.1 3.4 %all-to-all-start.2 = ((f32[8,40,128]{2,1,0:T(8,128)}), f32[8,40,128]{2,1,0:T(8,128)S(1)}, u32[]{:S(2)}, u32[]{:S(2)}) async-start(f32[8,40,128]{2,1,0:T(8,128)} %broadcast_in_dim.10), calls=%async_computation.2 | async-start | bytes 327680 | tf_op jit(solution)/shard_map/all_to_all | solution.py:259
  146.1 1.0 copy.134
  147.1 1.0 copy.135
  148.1 4.8 %all-to-all-done.2 = f32[8,40,128]{2,1,0:T(8,128)S(1)} async-done(((f32[8,40,128]{2,1,0:T(8,128)}), f32[8,40,128]{2,1,0:T(8,128)S(1)}, u32[]{:S(2)}, u32[]{:S(2)}) %all-to-all-start.2) | async-done | bytes 163872 | tf_op jit(solution)/shard_map/all_to_all | solution.py:259
  152.9 0.7 slice_multiply_fusion
  153.6 0.6 slice_multiply_fusion.2
  (120 shorter events, 6.5 us)
Async XLA Ops:
  0.6 10.2 %copy-start.4 = (f32[2,64,128]{2,1,0:T(8,128)S(1)}, f32[2,64,128]{2,1,0:T(8,128)}, u32[]{:S(2)}) copy-start(f32[2,64,128]{2,1,0:T(8,128)} %param.13) | copy-start | bytes 196612
  0.6 10.2 %copy-start.3 = (f32[2,64,128]{2,1,0:T(8,128)S(1)}, f32[2,64,128]{2,1,0:T(8,128)}, u32[]{:S(2)}) copy-start(f32[2,64,128]{2,1,0:T(8,128)} %param.14) | copy-start | bytes 196612
  2.6 11.9 %all-to-all-start = ((s32[4,2,4]{2,1,0:T(2,128)}), s32[4,2,4]{2,1,0:T(2,128)S(1)}, u32[]{:S(2)}, u32[]{:S(2)}) async-start(s32[4,2,4]{2,1,0:T(2,128)} %bitcast.177), calls=%async_computation | async-start | bytes 8192 | tf_op jit(solution)/shard_map/all_to_all | solution.py:301
  10.8 2.2 %copy-start.5 = (f32[16,2,128]{2,1,0:T(2,128)S(1)}, f32[16,2,128]{2,1,0:T(2,128)}, u32[]{:S(2)}) copy-start(f32[16,2,128]{2,1,0:T(2,128)} %param.15) | copy-start | bytes 49156
  16.9 14.0 %collective-permute-start.2 = (bf16[2,264,128]{2,1,0:T(8,128)(2,1)S(1)}, bf16[2,264,128]{2,1,0:T(8,128)(2,1)S(1)}, u32[]{:S(2)}, u32[]{:S(2)}) collective-permute-start(bf16[2,264,128]{2,1,0:T(8,128)(2,1)S(1)} %get-tuple-element.100), channel_id=1, source_target_pairs={{0,12},{1,13},{2,14},{3,15},{16,28},{17,29},{18,30},{19,31}} | collective-permute-start | bytes 405512 | tf_op jit(solution)/shard_map/ppermute | solution.py:322
  22.5 9.7 %collective-permute-start.1 = (bf16[2,264,128]{2,1,0:T(8,128)(2,1)S(1)}, bf16[2,264,128]{2,1,0:T(8,128)(2,1)S(1)}, u32[]{:S(2)}, u32[]{:S(2)}) collective-permute-start(bf16[2,264,128]{2,1,0:T(8,128)(2,1)S(1)} %get-tuple-element.99), channel_id=1, source_target_pairs={{0,8},{4,12},{1,9},{5,13},{2,10},{6,14},{3,11},{7,15},{16,24},{20,... | collective-permute-start | bytes 405512 | tf_op jit(solution)/shard_map/ppermute | solution.py:322
  23.8 8.5 %collective-permute-start = (bf16[2,264,128]{2,1,0:T(8,128)(2,1)S(1)}, bf16[2,264,128]{2,1,0:T(8,128)(2,1)S(1)}, u32[]{:S(2)}, u32[]{:S(2)}) collective-permute-start(bf16[2,264,128]{2,1,0:T(8,128)(2,1)S(1)} %get-tuple-element.98), channel_id=1, source_target_pairs={{0,4},{4,8},{8,12},{1,5},{5,9},{9,13},{2,6},{6,10},{10,14},{3,7},{... | collective-permute-start | bytes 405512 | tf_op jit(solution)/shard_map/ppermute | solution.py:322
  28.1 43.0 %collective-permute-start.5 = (bf16[2,264,128]{2,1,0:T(8,128)(2,1)S(1)}, bf16[2,264,128]{2,1,0:T(8,128)(2,1)S(1)}, u32[]{:S(2)}, u32[]{:S(2)}) collective-permute-start(bf16[2,264,128]{2,1,0:T(8,128)(2,1)S(1)} %get-tuple-element.103), channel_id=1, source_target_pairs={{0,12},{1,13},{2,14},{3,15},{16,28},{17,29},{18,30},{19,31}} | collective-permute-start | bytes 405512 | tf_op jit(solution)/shard_map/ppermute | solution.py:322
  29.4 43.1 %collective-permute-start.4 = (bf16[2,264,128]{2,1,0:T(8,128)(2,1)S(1)}, bf16[2,264,128]{2,1,0:T(8,128)(2,1)S(1)}, u32[]{:S(2)}, u32[]{:S(2)}) collective-permute-start(bf16[2,264,128]{2,1,0:T(8,128)(2,1)S(1)} %get-tuple-element.102), channel_id=1, source_target_pairs={{0,8},{4,12},{1,9},{5,13},{2,10},{6,14},{3,11},{7,15},{16,24},{20,... | collective-permute-start | bytes 405512 | tf_op jit(solution)/shard_map/ppermute | solution.py:322
  30.9 41.6 %collective-permute-start.3 = (bf16[2,264,128]{2,1,0:T(8,128)(2,1)S(1)}, bf16[2,264,128]{2,1,0:T(8,128)(2,1)S(1)}, u32[]{:S(2)}, u32[]{:S(2)}) collective-permute-start(bf16[2,264,128]{2,1,0:T(8,128)(2,1)S(1)} %get-tuple-element.101), channel_id=1, source_target_pairs={{0,4},{4,8},{8,12},{1,5},{5,9},{9,13},{2,6},{6,10},{10,14},{3,7},{... | collective-permute-start | bytes 405512 | tf_op jit(solution)/shard_map/ppermute | solution.py:322
  67.1 1.3 copy-start.2
  68.6 38.8 %collective-permute-start.6 = (bf16[2,256,128]{2,1,0:T(8,128)(2,1)S(1)}, bf16[2,256,128]{2,1,0:T(8,128)(2,1)S(1)}, u32[]{:S(2)}, u32[]{:S(2)}) collective-permute-start(bf16[2,256,128]{2,1,0:T(8,128)(2,1)S(1)} %get-tuple-element.68), channel_id=1, source_target_pairs={{4,0},{8,4},{12,8},{5,1},{9,5},{13,9},{6,2},{10,6},{14,10},{7,3},{... | collective-permute-start | bytes 393224 | tf_op jit(solution)/shard_map/ppermute | solution.py:325
  69.9 37.5 %collective-permute-start.7 = (bf16[2,256,128]{2,1,0:T(8,128)(2,1)S(1)}, bf16[2,256,128]{2,1,0:T(8,128)(2,1)S(1)}, u32[]{:S(2)}, u32[]{:S(2)}) collective-permute-start(bf16[2,256,128]{2,1,0:T(8,128)(2,1)S(1)} %get-tuple-element.67), channel_id=1, source_target_pairs={{8,0},{12,4},{9,1},{13,5},{10,2},{14,6},{11,3},{15,7},{24,16},{28,... | collective-permute-start | bytes 393224 | tf_op jit(solution)/shard_map/ppermute | solution.py:325
  71.2 36.2 %collective-permute-start.8 = (bf16[2,256,128]{2,1,0:T(8,128)(2,1)S(1)}, bf16[2,256,128]{2,1,0:T(8,128)(2,1)S(1)}, u32[]{:S(2)}, u32[]{:S(2)}) collective-permute-start(bf16[2,256,128]{2,1,0:T(8,128)(2,1)S(1)} %get-tuple-element.66), channel_id=1, source_target_pairs={{12,0},{13,1},{14,2},{15,3},{28,16},{29,17},{30,18},{31,19}} | collective-permute-start | bytes 393224 | tf_op jit(solution)/shard_map/ppermute | solution.py:325
  74.2 33.2 %copy-start.6 = (f32[1,32,128]{2,1,0:T(8,128)S(1)}, f32[1,32,128]{2,1,0:T(8,128)}, u32[]{:S(2)}) copy-start(f32[1,32,128]{2,1,0:T(8,128)} %get-tuple-element.33) | copy-start | bytes 49156
  74.2 33.2 %copy-start.7 = (f32[1,32,128]{2,1,0:T(8,128)S(1)}, f32[1,32,128]{2,1,0:T(8,128)}, u32[]{:S(2)}) copy-start(f32[1,32,128]{2,1,0:T(8,128)} %get-tuple-element.34) | copy-start | bytes 49156
  107.3 5.0 %copy-start.1 = (f32[1,1280,128]{2,1,0:T(8,128)S(1)}, f32[1,1280,128]{2,1,0:T(8,128)}, u32[]{:S(2)}) copy-start(f32[1,1280,128]{2,1,0:T(8,128)} %get-tuple-element.37) | copy-start | bytes 1966084
  107.3 5.1 %copy-start = (f32[1,1280,128]{2,1,0:T(8,128)S(1)}, f32[1,1280,128]{2,1,0:T(8,128)}, u32[]{:S(2)}) copy-start(f32[1,1280,128]{2,1,0:T(8,128)} %get-tuple-element.38) | copy-start | bytes 1966084
  108.3 13.4 %collective-permute-start.10 = (f32[2,2,8,128]{3,2,1,0:T(8,128)S(1)}, f32[2,2,8,128]{3,2,1,0:T(8,128)S(1)}, u32[]{:S(2)}, u32[]{:S(2)}) collective-permute-start(f32[2,2,8,128]{3,2,1,0:T(8,128)S(1)} %get-tuple-element.85), channel_id=1, source_target_pairs={{8,0},{12,4},{9,1},{13,5},{10,2},{14,6},{11,3},{15,7},{24,16},{28,... | collective-permute-start | bytes 49160 | tf_op jit(solution)/shard_map/ppermute | solution.py:325
  109.5 15.6 %collective-permute-start.11 = (f32[2,2,8,128]{3,2,1,0:T(8,128)S(1)}, f32[2,2,8,128]{3,2,1,0:T(8,128)S(1)}, u32[]{:S(2)}, u32[]{:S(2)}) collective-permute-start(f32[2,2,8,128]{3,2,1,0:T(8,128)S(1)} %get-tuple-element.84), channel_id=1, source_target_pairs={{12,0},{13,1},{14,2},{15,3},{28,16},{29,17},{30,18},{31,19}} | collective-permute-start | bytes 49160 | tf_op jit(solution)/shard_map/ppermute | solution.py:325
  110.8 14.3 %collective-permute-start.9 = (f32[2,2,8,128]{3,2,1,0:T(8,128)S(1)}, f32[2,2,8,128]{3,2,1,0:T(8,128)S(1)}, u32[]{:S(2)}, u32[]{:S(2)}) collective-permute-start(f32[2,2,8,128]{3,2,1,0:T(8,128)S(1)} %get-tuple-element.83), channel_id=1, source_target_pairs={{4,0},{8,4},{12,8},{5,1},{9,5},{13,9},{6,2},{10,6},{14,10},{7,3},{... | collective-permute-start | bytes 49160 | tf_op jit(solution)/shard_map/ppermute | solution.py:325
  112.5 0.7 copy-start.8
  112.5 0.7 copy-start.9
  113.3 20.0 %collective-permute-start.12 = (bf16[2,256,128]{2,1,0:T(8,128)(2,1)S(1)}, bf16[2,256,128]{2,1,0:T(8,128)(2,1)S(1)}, u32[]{:S(2)}, u32[]{:S(2)}) collective-permute-start(bf16[2,256,128]{2,1,0:T(8,128)(2,1)S(1)} %get-tuple-element.63), channel_id=1, source_target_pairs={{4,0},{8,4},{12,8},{5,1},{9,5},{13,9},{6,2},{10,6},{14,10},{7,3},{... | collective-permute-start | bytes 393224 | tf_op jit(solution)/shard_map/ppermute | solution.py:325
  114.6 25.5 %collective-permute-start.13 = (bf16[2,256,128]{2,1,0:T(8,128)(2,1)S(1)}, bf16[2,256,128]{2,1,0:T(8,128)(2,1)S(1)}, u32[]{:S(2)}, u32[]{:S(2)}) collective-permute-start(bf16[2,256,128]{2,1,0:T(8,128)(2,1)S(1)} %get-tuple-element.65), channel_id=1, source_target_pairs={{8,0},{12,4},{9,1},{13,5},{10,2},{14,6},{11,3},{15,7},{24,16},{28,... | collective-permute-start | bytes 393224 | tf_op jit(solution)/shard_map/ppermute | solution.py:325
  121.7 18.4 %collective-permute-start.14 = (bf16[2,256,128]{2,1,0:T(8,128)(2,1)S(1)}, bf16[2,256,128]{2,1,0:T(8,128)(2,1)S(1)}, u32[]{:S(2)}, u32[]{:S(2)}) collective-permute-start(bf16[2,256,128]{2,1,0:T(8,128)(2,1)S(1)} %get-tuple-element.64), channel_id=1, source_target_pairs={{12,0},{13,1},{14,2},{15,3},{28,16},{29,17},{30,18},{31,19}} | collective-permute-start | bytes 393224 | tf_op jit(solution)/shard_map/ppermute | solution.py:325
  125.9 15.4 %all-to-all-start.1 = ((f32[8,40,128]{2,1,0:T(8,128)}), f32[8,40,128]{2,1,0:T(8,128)S(1)}, u32[]{:S(2)}, u32[]{:S(2)}) async-start(f32[8,40,128]{2,1,0:T(8,128)} %bitcast.83), calls=%async_computation.1 | async-start | bytes 327680 | tf_op jit(solution)/shard_map/all_to_all | solution.py:257
  142.1 10.9 %all-to-all-start.2 = ((f32[8,40,128]{2,1,0:T(8,128)}), f32[8,40,128]{2,1,0:T(8,128)S(1)}, u32[]{:S(2)}, u32[]{:S(2)}) async-start(f32[8,40,128]{2,1,0:T(8,128)} %broadcast_in_dim.10), calls=%async_computation.2 | async-start | bytes 327680 | tf_op jit(solution)/shard_map/all_to_all | solution.py:259
